TPU v7x, 512 devices: a whole 4x8x8 slice. The times are simulated.
512 devices in a mesh: tm: 32 (over z_hi, x, core), space: 16 (over y, z_lo).
Axes of the slice: x: 4, y: 8, z: 8 (z_hi: 4, z_lo: 2; z = z_hi * 2 + z_lo), core: 2. Of those that a mesh axis runs over, the one named last changes fastest.
Arguments:
- initial_density: float32 [384, 512], P('space'), may hold values from 0.5 to 2
- terminal_cost: float32 [384, 512], P('space'), may hold values from -1.2 to 1.2
- running_cost: float32 [384, 512], P('space'), may hold values from -0.3 to 0.3
- discount_rate: float32 [384, 512], P('space'), may hold values from 0.003 to 0.5
- slice_steps: int32 [32], replicated, may hold values from 4 to 8
Outputs:
- density_path: float32 [32, 384, 512], P('tm', 'space')
- value_path: float32 [32, 384, 512], P('tm', 'space')
All inputs are finite; a program needn't handle non-finite values.
Results may differ from a plain program's by a relative error of at most 0.0003.
Values sent between devices are 32-bit elements; how exact they have to be, the bound alone decides.
No kernel may reach another device: no remote copies, remote signals or barrier semaphores. Data moves between devices by JAX's collectives and lax.ppermute only.
A program may use at most 64 MiB of HBM per device.

v0:
```python
import jax
import jax.numpy as jnp
from jax import lax
from jax.sharding import Mesh
from jax.sharding import PartitionSpec as P

K = 8
ITERS = 2
TM = ("tm_0", "tm_1", "tm_2")


time_step = 0.05
diffusion = 2.0
coupling = 0.1


def extended(block, sides, width):
    for axis, dim in sides:
        count = lax.axis_size(axis)
        forward = [(i, i + 1) for i in range(count - 1)]
        forward.append((count - 1, 0))
        backward = [(target, source) for source, target in forward]
        low = lax.ppermute(
            lax.slice_in_dim(block, block.shape[dim] - width, None, axis=dim), axis, forward
        )
        high = lax.ppermute(lax.slice_in_dim(block, 0, width, axis=dim), axis, backward)
        block = jnp.concatenate([low, block, high], axis=dim)
    return block


def filled_with(shard, identity):
    return jax.tree.map(
        lambda a, e: jnp.broadcast_to(jnp.asarray(e, a.dtype), a.shape), shard, identity
    )


def prefix_by_axis(shard, axes, combine, identity, reverse):
    before = start = filled_with(shard, identity)
    running = shard
    for axis in reversed(axes):
        devices, index = (lax.axis_size(axis), lax.axis_index(axis))
        pieces = jax.tree.map(lambda part: lax.all_gather(part, axis), running)
        inside, running = (start, start)
        for k in reversed(range(devices)) if reverse else range(devices):
            passed = k > index if reverse else k < index
            running = combine(running, jax.tree.map(lambda part: part[k], pieces))
            inside = jax.tree.map(lambda new, old: jnp.where(passed, new, old), running, inside)
        before = combine(inside, before)
    return before


def laplace(padded):
    middle = padded[1:-1]
    return (
        padded[2:] + padded[:-2] + jnp.roll(middle, 1, 1) + jnp.roll(middle, -1, 1) - 4.0 * middle
    )


def slopes(padded):
    middle = padded[1:-1]
    return (
        0.5 * (padded[2:] - padded[:-2]),
        0.5 * (jnp.roll(middle, -1, 1) - jnp.roll(middle, 1, 1)),
    )


def value_step(padded, source):
    slope_across, slope_along = slopes(padded)
    hamilton = 0.5 * (slope_across * slope_across + slope_along * slope_along)
    return padded[1:-1] + time_step * (diffusion * laplace(padded) - hamilton + source)


def density_step(density, value):
    slope_across, slope_along = slopes(value)
    flux_across = density * slope_across
    flux_along = density * slope_along
    inner = flux_along[1:-1]
    divergence = 0.5 * (flux_across[2:] - flux_across[:-2]) + 0.5 * (
        jnp.roll(inner, -1, 1) - jnp.roll(inner, 1, 1)
    )
    return density[1:-1] + time_step * (diffusion * laplace(density) + divergence)


def trim_rows(field, width):
    return field[width : field.shape[0] - width]


def fine_deep(density_start, value_end, running_cost, own_steps):
    reach = 2 * K + 1
    padded = extended(jnp.stack([value_end, density_start, running_cost]), (("space", 1),), reach)
    source = padded[2] + coupling * padded[1]
    value_now = padded[0]
    stored = [value_now]
    for substep in range(K):
        active = substep >= K - own_steps
        value_now = jnp.where(
            active, value_step(value_now, trim_rows(source, substep + 1)), trim_rows(value_now, 1)
        )
        stored.append(value_now)
    density_now = trim_rows(padded[1], reach - K)
    for substep in range(K):
        active = substep < own_steps
        density_now = jnp.where(
            active,
            density_step(density_now, trim_rows(stored[K - substep], 2 * substep)),
            trim_rows(density_now, 1),
        )
    return (density_now, trim_rows(value_now, K + 1))


def compose(earlier, latter):
    return (latter[0] * earlier[0], latter[0] * earlier[1] + latter[1])


def on_device(initial_density, terminal_cost, running_cost, discount_rate, slice_steps):
    own_index = lax.axis_index(TM)
    indices = jnp.arange(slice_steps.shape[0], dtype=jnp.int32)
    own_steps = jnp.sum(jnp.where(indices == own_index, slice_steps, 0))
    duration = time_step * own_steps.astype(jnp.float32)
    damping = jnp.exp(-discount_rate * duration)
    ones_field = jnp.ones_like(damping)
    zeros_field = jnp.zeros_like(damping)
    before = time_step * jnp.sum(jnp.where(indices < own_index, slice_steps, 0)).astype(jnp.float32)
    after = time_step * jnp.sum(jnp.where(indices > own_index, slice_steps, 0)).astype(jnp.float32)
    density_now = jnp.exp(-discount_rate * before) * initial_density
    value_now = (
        jnp.exp(-discount_rate * after) * terminal_cost
        - jnp.expm1(-discount_rate * after) / discount_rate * running_cost
    )
    for iteration in range(ITERS):
        fine_density, fine_value = fine_deep(density_now, value_now, running_cost, own_steps)
        density_terms = fine_density - damping * density_now
        value_terms = fine_value - damping * value_now
        factors, offsets = prefix_by_axis(
            (damping, density_terms), TM, compose, (ones_field, zeros_field), False
        )
        density_now = factors * initial_density + offsets
        factors, offsets = prefix_by_axis(
            (damping, value_terms), TM, compose, (ones_field, zeros_field), True
        )
        value_now = factors * terminal_cost + offsets
    return (density_now[None], value_now[None])


def solution(mesh):
    finer = Mesh(
        mesh.devices.reshape(4, 4, 2, mesh.shape["space"]), ("tm_0", "tm_1", "tm_2", "space")
    )
    placed = (P("space", None), P("space", None), P("space", None), P("space", None), P())
    return jax.shard_map(
        on_device,
        mesh=finer,
        in_specs=placed,
        out_specs=(P(TM, "space", None), P(TM, "space", None)),
        check_vma=False,
    )
```

profile of v0, /device:TPU:94, one launch (start us, length us, event | category | flops | bytes accessed | tf_op | source)
XLA Modules:
  0.0 211.0 jit_solution(1450050056270475092)
XLA Ops:
  0.7 0.6 copy-done.4
  1.3 0.7 fusion.303
  3.4 0.9 multiply_subtract_fusion
  4.4 3.8 %collective-permute-start = (f32[3,17,512]{2,1,0:T(8,128)S(1)}, f32[3,17,512]{2,1,0:T(8,128)S(1)}, u32[]{:S(2)}, u32[]{:S(2)}) collective-permute-start(f32[3,17,512]{2,1,0:T(8,128)S(1)} %get-tuple-element.46), channel_id=1, source_target_pairs={{0,1},{1,2},{2,3},{3,4},{4,5},{5,6},{6,7},{7,8},{8,9},{9,10},{10,1... | collective-permute-start | bytes 313352 | tf_op jit(solution)/shard_map/ppermute | solution.py:23
  8.2 2.1 collective-permute-start.1
  16.8 0.7 collective-permute-done.1
  20.9 0.2 fusion.117
  21.5 0.2 fusion.119
  25.4 0.6 copy-done.3
  26.0 2.0 all-gather
  28.2 1.9 all-gather.2
  30.0 1.9 all-gather.1
  31.9 12.3 %all_gather.44 = f32[4,24,512]{2,1,0:T(8,128)S(1)} all-gather(f32[1,24,512]{2,1,0:T(8,128)S(1)} %get-tuple-element.152), channel_id=1, replica_groups=mesh['tm_0'=4,'tm_1'=4,'tm_2'=2,'space'=16] {'tm_1'}, dimensions={0}, use_global_device_ids=true | all-gather | bytes 245760 | tf_op jit(solution)/shard_map/all_gather | solution.py:42
  44.2 12.1 %all_gather.97 = f32[4,24,512]{2,1,0:T(8,128)S(1)} all-gather(f32[1,24,512]{2,1,0:T(8,128)S(1)} %get-tuple-element.150), channel_id=1, replica_groups=mesh['tm_0'=4,'tm_1'=4,'tm_2'=2,'space'=16] {'tm_1'}, dimensions={0}, use_global_device_ids=true | all-gather | bytes 245760 | tf_op jit(solution)/shard_map/all_gather | solution.py:42
  56.3 20.0 %all_gather.46 = f32[4,24,512]{2,1,0:T(8,128)S(1)} all-gather(f32[1,24,512]{2,1,0:T(8,128)S(1)} %get-tuple-element.41), channel_id=1, replica_groups=mesh['tm_0'=4,'tm_1'=4,'tm_2'=2,'space'=16] {'tm_0'}, dimensions={0}, use_global_device_ids=true | all-gather | bytes 245760 | tf_op jit(solution)/shard_map/all_gather | solution.py:42
  76.4 14.2 %all_gather.98 = f32[4,24,512]{2,1,0:T(8,128)S(1)} all-gather(f32[1,24,512]{2,1,0:T(8,128)S(1)} %get-tuple-element.42), channel_id=1, replica_groups=mesh['tm_0'=4,'tm_1'=4,'tm_2'=2,'space'=16] {'tm_0'}, dimensions={0}, use_global_device_ids=true | all-gather | bytes 245760 | tf_op jit(solution)/shard_map/all_gather | solution.py:42
  90.6 14.1 %all_gather.45 = f32[4,24,512]{2,1,0:T(8,128)S(1)} all-gather(f32[1,24,512]{2,1,0:T(8,128)S(1)} %get-tuple-element.43), channel_id=1, replica_groups=mesh['tm_0'=4,'tm_1'=4,'tm_2'=2,'space'=16] {'tm_0'}, dimensions={0}, use_global_device_ids=true | all-gather | bytes 245760 | tf_op jit(solution)/shard_map/all_gather | solution.py:42
  104.7 12.1 %all_gather.101 = f32[4,24,512]{2,1,0:T(8,128)S(1)} all-gather(f32[1,24,512]{2,1,0:T(8,128)S(1)} %get-tuple-element.151), channel_id=1, replica_groups=mesh['tm_0'=4,'tm_1'=4,'tm_2'=2,'space'=16] {'tm_1'}, dimensions={0}, use_global_device_ids=true | all-gather | bytes 245760 | tf_op jit(solution)/shard_map/all_gather | solution.py:42
  116.8 14.3 %all_gather.102 = f32[4,24,512]{2,1,0:T(8,128)S(1)} all-gather(f32[1,24,512]{2,1,0:T(8,128)S(1)} %multiply_add_fusion.2), channel_id=1, replica_groups=mesh['tm_0'=4,'tm_1'=4,'tm_2'=2,'space'=16] {'tm_0'}, dimensions={0}, use_global_device_ids=true | all-gather | bytes 245760 | tf_op jit(solution)/shard_map/all_gather | solution.py:42
  131.5 4.9 %collective-permute-start.2 = (f32[3,17,512]{2,1,0:T(8,128)S(1)}, f32[3,17,512]{2,1,0:T(8,128)S(1)}, u32[]{:S(2)}, u32[]{:S(2)}) collective-permute-start(f32[3,17,512]{2,1,0:T(8,128)S(1)} %get-tuple-element.44), channel_id=1, source_target_pairs={{0,1},{1,2},{2,3},{3,4},{4,5},{5,6},{6,7},{7,8},{8,9},{9,10},{10,1... | collective-permute-start | bytes 313352 | tf_op jit(solution)/shard_map/ppermute | solution.py:23
  136.4 1.9 collective-permute-start.3
  138.3 0.7 collective-permute-done.2
  139.0 6.5 %collective-permute-done.3 = f32[3,17,512]{2,1,0:T(8,128)S(1)} collective-permute-done((f32[3,17,512]{2,1,0:T(8,128)S(1)}, f32[3,17,512]{2,1,0:T(8,128)S(1)}, u32[]{:S(2)}, u32[]{:S(2)}) %collective-permute-start.3) | collective-permute-done | bytes 104480 | tf_op jit(solution)/shard_map/ppermute | solution.py:26
  148.9 0.2 fusion.125
  153.6 1.9 all-gather.3
  155.5 1.9 all-gather.4
  157.4 12.1 %all_gather.105 = f32[4,24,512]{2,1,0:T(8,128)S(1)} all-gather(f32[1,24,512]{2,1,0:T(8,128)S(1)} %get-tuple-element.121), channel_id=1, replica_groups=mesh['tm_0'=4,'tm_1'=4,'tm_2'=2,'space'=16] {'tm_1'}, dimensions={0}, use_global_device_ids=true | all-gather | bytes 245760 | tf_op jit(solution)/shard_map/all_gather | solution.py:42
  169.5 12.1 %all_gather.109 = f32[4,24,512]{2,1,0:T(8,128)S(1)} all-gather(f32[1,24,512]{2,1,0:T(8,128)S(1)} %get-tuple-element.120), channel_id=1, replica_groups=mesh['tm_0'=4,'tm_1'=4,'tm_2'=2,'space'=16] {'tm_1'}, dimensions={0}, use_global_device_ids=true | all-gather | bytes 245760 | tf_op jit(solution)/shard_map/all_gather | solution.py:42
  181.7 13.9 %all_gather.110 = f32[4,24,512]{2,1,0:T(8,128)S(1)} all-gather(f32[1,24,512]{2,1,0:T(8,128)S(1)} %get-tuple-element.39), channel_id=1, replica_groups=mesh['tm_0'=4,'tm_1'=4,'tm_2'=2,'space'=16] {'tm_0'}, dimensions={0}, use_global_device_ids=true | all-gather | bytes 245760 | tf_op jit(solution)/shard_map/all_gather | solution.py:42
  195.6 0.7 fusion.233
  196.3 13.9 %all_gather.106 = f32[4,24,512]{2,1,0:T(8,128)S(1)} all-gather(f32[1,24,512]{2,1,0:T(8,128)S(1)} %get-tuple-element.40), channel_id=1, replica_groups=mesh['tm_0'=4,'tm_1'=4,'tm_2'=2,'space'=16] {'tm_0'}, dimensions={0}, use_global_device_ids=true | all-gather | bytes 245760 | tf_op jit(solution)/shard_map/all_gather | solution.py:42
  210.3 0.7 fusion.242
  (200 shorter events, 15.3 us)
Async XLA Ops:
  0.6 0.7 copy-start.4
  3.4 0.9 copy-start
  4.4 12.4 %collective-permute-start = (f32[3,17,512]{2,1,0:T(8,128)S(1)}, f32[3,17,512]{2,1,0:T(8,128)S(1)}, u32[]{:S(2)}, u32[]{:S(2)}) collective-permute-start(f32[3,17,512]{2,1,0:T(8,128)S(1)} %get-tuple-element.46), channel_id=1, source_target_pairs={{0,1},{1,2},{2,3},{3,4},{4,5},{5,6},{6,7},{7,8},{8,9},{9,10},{10,1... | collective-permute-start | bytes 313352 | tf_op jit(solution)/shard_map/ppermute | solution.py:23
  8.2 9.3 %collective-permute-start.1 = (f32[3,17,512]{2,1,0:T(8,128)S(1)}, f32[3,17,512]{2,1,0:T(8,128)S(1)}, u32[]{:S(2)}, u32[]{:S(2)}) collective-permute-start(f32[3,17,512]{2,1,0:T(8,128)S(1)} %get-tuple-element.47), channel_id=1, source_target_pairs={{1,0},{2,1},{3,2},{4,3},{5,4},{6,5},{7,6},{8,7},{9,8},{10,9},{11,1... | collective-permute-start | bytes 313352 | tf_op jit(solution)/shard_map/ppermute | solution.py:26
  25.2 0.8 copy-start.3
  26.0 2.0 copy-start.1
  116.8 14.3 %copy-start.2 = (f32[24,512]{1,0:T(8,128)S(1)}, f32[24,512]{1,0:T(8,128)}, u32[]{:S(2)}) copy-start(f32[24,512]{1,0:T(8,128)} %param.6) | copy-start | bytes 147460
  131.5 7.5 %collective-permute-start.2 = (f32[3,17,512]{2,1,0:T(8,128)S(1)}, f32[3,17,512]{2,1,0:T(8,128)S(1)}, u32[]{:S(2)}, u32[]{:S(2)}) collective-permute-start(f32[3,17,512]{2,1,0:T(8,128)S(1)} %get-tuple-element.44), channel_id=1, source_target_pairs={{0,1},{1,2},{2,3},{3,4},{4,5},{5,6},{6,7},{7,8},{8,9},{9,10},{10,1... | collective-permute-start | bytes 313352 | tf_op jit(solution)/shard_map/ppermute | solution.py:23
  136.4 9.1 %collective-permute-start.3 = (f32[3,17,512]{2,1,0:T(8,128)S(1)}, f32[3,17,512]{2,1,0:T(8,128)S(1)}, u32[]{:S(2)}, u32[]{:S(2)}) collective-permute-start(f32[3,17,512]{2,1,0:T(8,128)S(1)} %get-tuple-element.45), channel_id=1, source_target_pairs={{1,0},{2,1},{3,2},{4,3},{5,4},{6,5},{7,6},{8,7},{9,8},{10,9},{11,1... | collective-permute-start | bytes 313352 | tf_op jit(solution)/shard_map/ppermute | solution.py:26
where the time goes:
time: 212 us; the launch traced here: 211 us
  blocking collectives  161 us (76%)
  starting transfers between devices  12.7 us (6%)
  local copies, waits for them, and re-layouts  11.6 us (5%)
  between operations  9.52 us (4%)
  other arithmetic  8.52 us (4%)
  waiting for transfers between devices  7.93 us (4%)
    all_gather x16, blocking collectives, prefix_by_axis(): pieces = jax.tree.map(lambda part: lax.all_gather(part, axis), running)  161 us
    ppermute x2, starting transfers between devices, extended(): lax.ppermute(lax.slice_in_dim(block, block.shape[dim] - width, None, axis...  8.67 us
    ppermute x2, waiting for transfers between devices, extended(): lax.ppermute(lax.slice_in_dim(block, 0, width, axis=dim), axis, backward)  7.2 us
    slice x60, local copies, waits for them, and re-layouts, laplace(): jnp.roll(middle, 1, 1)  4.96 us
  transfers between devices with their start and end apart: 4, of which 3 were waited for; matrix products, arithmetic and copies ran while one was open for 0% of the time, Pallas kernels for 0%

commit v1 on v0

v1 whole, which is shorter than its diff:
```python
import jax
import jax.numpy as jnp
from jax import lax
from jax.experimental import pallas as pl
from jax.experimental.pallas import tpu as pltpu
from jax.sharding import Mesh
from jax.sharding import PartitionSpec as P


K = 8
SLICES = 32
LEAST = 4
KINDS = K - LEAST + 1
TM = ("zh", "x", "c")
SPACE = ("y", "zl")

time_step = 0.05
diffusion = 2.0
coupling = 0.1

ROWS = 24
TILE_ROWS = 12
TILE_COLS = 32
LANES = 128
COL_AT = 48
FRAME1 = 88
FRAME2 = 56
SCALE = 16.0


def planes_of(ref, at, start, count):
    return [ref[(*at, pl.ds(start + k, 8, stride=count), slice(None))] for k in range(count)]


def put_planes(ref, at, start, planes):
    count = len(planes)
    for k, plane in enumerate(planes):
        ref[(*at, pl.ds(start + k, 8, stride=count), slice(None))] = plane


def row_above(planes):
    return [pltpu.roll(planes[-1], 1, 0), *planes[:-1]]


def row_below(planes):
    return [*planes[1:], pltpu.roll(planes[0], 7, 0)]


def left(plane):
    return pltpu.roll(plane, 1, 1)


def right(plane):
    return pltpu.roll(plane, LANES - 1, 1)


def slope_planes(planes):
    up, down = row_above(planes), row_below(planes)
    slopes, sums = [], []
    for k, plane in enumerate(planes):
        west, east = left(plane), right(plane)
        slopes.append((down[k] - up[k], east - west))
        sums.append((up[k] + down[k]) + (west + east))
    return slopes, sums


def fine_pairs(order, steps, values, densities, cost, sources, across, along, out_value, out_density, spots):
    (value_at, value_n), (density_at, density_n) = spots

    def pair(number, carry):
        own = [order[2 * number], order[2 * number + 1]]
        trips = [steps[own[0]], steps[own[1]]]
        most = jnp.maximum(trips[0], trips[1])
        start = []
        for h in range(2):
            start.append(planes_of(values, (own[h],), value_at, value_n))
            held = planes_of(densities, (own[h],), value_at, value_n)
            for k in range(value_n):
                sources[h, k] = cost[k] + (0.5 / SCALE * coupling) * held[k]

        def put_slopes(h, q, slopes):
            put_planes(across, (h, q), value_at, [a for a, _ in slopes])
            put_planes(along, (h, q), value_at, [b for _, b in slopes])

        def value_step(q, now):
            result = []
            for h in range(2):
                active = q >= most - trips[h]
                keep = jnp.where(active, 1.0 - 4.0 * time_step * diffusion, 1.0)
                share = jnp.where(active, time_step * diffusion, 0.0)
                slopes, sums = slope_planes(now[h])
                put_slopes(h, q, slopes)
                result.append([
                    keep * plane + share * (sums[k] + (sources[h, k] - (slopes[k][0] * slopes[k][0] + slopes[k][1] * slopes[k][1])))
                    for k, plane in enumerate(now[h])
                ])
            return result

        now = lax.fori_loop(0, most, value_step, start)
        for h in range(2):
            put_slopes(h, most, slope_planes(now[h])[0])
            put_planes(out_value, (own[h],), value_at, now[h])

        def density_step(i, held):
            q = most - i
            result = []
            for h in range(2):
                active = i < trips[h]
                keep = jnp.where(active, 1.0 - 4.0 * time_step * diffusion, 1.0)
                share = jnp.where(active, time_step * diffusion, 0.0)
                a = planes_of(across, (h, q), density_at, density_n)
                b = planes_of(along, (h, q), density_at, density_n)
                here = held[h]
                twice = [plane + plane for plane in here]
                flux = [twice[k] * a[k] for k in range(density_n)]
                below = row_below([here[k] + flux[k] for k in range(density_n)])
                above = row_above([here[k] - flux[k] for k in range(density_n)])
                new = []
                for k in range(density_n):
                    drift = twice[k] * b[k]
                    around = (below[k] + above[k]) + (right(here[k] + drift) + left(here[k] - drift))
                    new.append(keep * here[k] + share * around)
                result.append(new)
            return result

        begin = [planes_of(densities, (own[h],), density_at, density_n) for h in range(2)]
        end = lax.fori_loop(0, most, density_step, begin)
        for h in range(2):
            put_planes(out_density, (own[h],), density_at, end[h])
        return carry

    lax.fori_loop(0, SLICES // 2, pair, 0)


def main_kernel(order, steps, core, own, low, high, far, message, field, factors, reliefs, cost, m0, u0, m1, u1, fm, fu, across, along, sources):
    for part in range(4):

        @pl.when(core[0] == 0)
        def _(part=part):
            field[part, 6:16] = far[part, 6:16]
            field[part, 16:40] = low[part]
            field[part, 40:64] = own[part]
            field[part, 64:86] = high[part, 0:22]

        @pl.when(core[0] != 0)
        def _(part=part):
            field[part, 6:28] = low[part, 2:24]
            field[part, 28:52] = own[part]
            field[part, 52:76] = high[part]
            field[part, 76:86] = far[part, 0:10]

    rate, running = field[3], field[2]
    quotient = running / rate
    for kind in range(KINDS):
        factor = jnp.exp(rate * (-time_step * (LEAST + kind)))
        factors[kind] = factor
        reliefs[kind] = (1.0 - factor) * quotient * (1.0 / SCALE)
    cost[...] = running * (0.5 / SCALE)

    def opening(j, now):
        density, value = now
        back = SLICES - 1 - j
        m0[j] = density
        u0[back] = value
        kind = steps[back] - LEAST
        return factors[steps[j] - LEAST] * density, factors[kind] * value + reliefs[kind]

    lax.fori_loop(0, SLICES, opening, (field[0], field[1] * (1.0 / SCALE)))

    fine_pairs(order, steps, u0, m0, planes_of(cost, (), 6, 10), sources, across, along, fu, fm, ((6, 10), (14, 8)))

    inner = pl.ds(16, FRAME2)

    def first_sweep(j, now):
        density, value = now
        back = SLICES - 1 - j
        m1[j] = density
        u1[back] = value
        density = factors[steps[j] - LEAST, inner] * (density - m0[j, inner]) + fm[j, inner]
        value = factors[steps[back] - LEAST, inner] * (value - u0[back, inner]) + fu[back, inner]
        return density, value

    lax.fori_loop(0, SLICES, first_sweep, (field[0, inner], field[1, inner] * (1.0 / SCALE)))

    fine_pairs(order, steps, u1, m1, planes_of(cost, (), 22, 6), sources, across, along, fu, fm, ((6, 6), (16, 4)))

    tile, wide = pl.ds(24, 16), pl.ds(40, 16)
    lane = lax.broadcasted_iota(jnp.int32, (8, LANES), 1)
    for_density, first_rows = lane < 64, (lane % 64) < 32

    def second_sweep(j, now):
        density, value = now
        back = SLICES - 1 - j
        u0[back, 0:16] = value
        m0[j, 0:16] = density
        density = factors[steps[j] - LEAST, wide] * (density - m1[j, tile]) + fm[j, tile]
        value = factors[steps[back] - LEAST, wide] * (value - u1[back, tile]) + fu[back, tile]
        return density, value

    lax.fori_loop(0, SLICES, second_sweep, (field[0, wide], field[1, wide] * (1.0 / SCALE)))

    def moved(plane, lane_now):
        return pltpu.roll(plane, (lane_now - COL_AT) % LANES, 1)

    def packed(j, carry):
        density = jnp.where(first_rows, moved(m0[j, 0:8], 0), moved(m0[j, 8:16], 32))
        value = SCALE * jnp.where(first_rows, moved(u0[j, 0:8], 64), moved(u0[j, 8:16], 96))
        message[j] = jnp.where(for_density, density, value)
        return carry

    lax.fori_loop(0, SLICES, packed, 0)


def window_kernel(place, *refs):
    blocks, (near, far) = refs[:8], refs[8:]
    shift, first = place[2], place[3]
    lane = lax.broadcasted_iota(jnp.int32, (ROWS, LANES), 1)
    for part in range(4):
        a = pltpu.roll(blocks[2 * part][...], shift, 1)
        b = pltpu.roll(blocks[2 * part + 1][...], shift, 1)
        window = jnp.where(lane < shift, a, b)
        near[part] = window

        @pl.when(first == 0)
        def _(window=window, part=part):
            far[part] = window[8:24]

        @pl.when(first != 0)
        def _(window=window, part=part):
            far[part] = window[0:16]


def gather_kernel(received, density, value):
    lane = lax.broadcasted_iota(jnp.int32, (8, LANES), 1)
    for column in range(4):
        for half in range(2):
            for out, base in ((density, 0), (value, 64)):
                for rows, block, begin in ((8, base, 0), (4, base + 32, 8)):
                    whole = None
                    for x in range(4):
                        source = received[column * 8 + x * 2 + half]
                        piece = pltpu.roll(source, (32 * x - block) % LANES, 1)
                        whole = piece if whole is None else jnp.where(lane >= 32 * x, piece, whole)
                    at = TILE_ROWS * half + begin
                    out[0, at : at + rows, LANES * column : LANES * (column + 1)] = whole[0:rows]


def vmem():
    return pl.BlockSpec(memory_space=pltpu.VMEM)


def smem():
    return pl.BlockSpec(memory_space=pltpu.SMEM)


def f32(*shape):
    return jax.ShapeDtypeStruct(shape, jnp.float32)


def windows(place, arrays):
    specs, operands = [], []
    for array in arrays:
        for which in range(2):
            specs.append(pl.BlockSpec((ROWS, LANES), lambda i, place, which=which: (0, place[which])))
            operands.append(array)
    return pl.pallas_call(
        window_kernel,
        out_shape=[f32(4, ROWS, LANES), f32(4, 16, LANES)],
        grid_spec=pltpu.PrefetchScalarGridSpec(
            num_scalar_prefetch=1,
            grid=(1,),
            in_specs=specs,
            out_specs=[
                pl.BlockSpec((4, ROWS, LANES), lambda i, place: (0, 0, 0)),
                pl.BlockSpec((4, 16, LANES), lambda i, place: (0, 0, 0)),
            ],
        ),
        name="windows",
    )(place, *operands)


def both_iterations(order, steps, core, own, low, high, far):
    scratch = [
        (4, FRAME1, LANES),
        (KINDS, FRAME1, LANES),
        (KINDS, FRAME1, LANES),
        (FRAME1, LANES),
        (SLICES, FRAME1, LANES),
        (SLICES, FRAME1, LANES),
        (SLICES, FRAME2, LANES),
        (SLICES, FRAME2, LANES),
        (SLICES, FRAME1, LANES),
        (SLICES, FRAME1, LANES),
        (2, K + 1, FRAME1, LANES),
        (2, K + 1, FRAME1, LANES),
        (2, 10, 8, LANES),
    ]
    return pl.pallas_call(
        main_kernel,
        out_shape=f32(SLICES, 8, LANES),
        in_specs=[smem(), smem(), smem(), vmem(), vmem(), vmem(), vmem()],
        out_specs=vmem(),
        scratch_shapes=[pltpu.VMEM(shape, jnp.float32) for shape in scratch],
        compiler_params=pltpu.CompilerParams(vmem_limit_bytes=32 * 2**20),
        name="both_iterations",
    )(order, steps, core, own, low, high, far)


def gathered(received):
    return pl.pallas_call(
        gather_kernel,
        out_shape=[f32(1, ROWS, 512), f32(1, ROWS, 512)],
        in_specs=[vmem()],
        out_specs=[vmem(), vmem()],
        name="gathered",
    )(received)


def from_offset(array, offset):
    count = 16
    return lax.ppermute(array, SPACE, [((i + offset) % count, i) for i in range(count)])


def on_device(initial_density, terminal_cost, running_cost, discount_rate, slice_steps):
    core = lax.axis_index("c")
    column = lax.axis_index("zh") * 4 + lax.axis_index("x")
    begin = (column * TILE_COLS - COL_AT) % 512
    first_block = begin // LANES
    shift = (LANES - begin % LANES) % LANES
    whole = (shift == 0).astype(jnp.int32)
    place = jnp.stack([first_block, (first_block + 1 - whole) % 4, shift, core]).astype(jnp.int32)
    own, edge = windows(place, (initial_density, terminal_cost, running_cost, discount_rate))
    low = from_offset(own, -1)
    high = from_offset(own, 1)
    hops = []
    for space in range(16):
        for c in range(2):
            source = (space - 2) % 16 if c == 0 else (space + 2) % 16
            hops.append((c * 16 + source, c * 16 + space))
    far = lax.ppermute(edge, ("c", *SPACE), hops)
    numbers = jnp.arange(SLICES, dtype=jnp.int32)
    ahead = (slice_steps[None, :] < slice_steps[:, None]) | ((slice_steps[None, :] == slice_steps[:, None]) & (numbers[None, :] < numbers[:, None]))
    rank = jnp.sum(ahead.astype(jnp.int32), axis=1)
    order = jnp.sum(jnp.where(rank[None, :] == numbers[:, None], numbers[None, :], 0), axis=1)
    message = both_iterations(order, slice_steps, core[None].astype(jnp.int32), own, low, high, far)
    received = lax.all_to_all(message, TM, 0, 0, tiled=True)
    return tuple(gathered(received))


def solution(mesh):
    finer = Mesh(mesh.devices.reshape(4, 4, 2, 8, 2), ("zh", "x", "c", "y", "zl"))
    placed = (P(SPACE, None), P(SPACE, None), P(SPACE, None), P(SPACE, None), P())
    return jax.shard_map(
        on_device,
        mesh=finer,
        in_specs=placed,
        out_specs=(P(TM, SPACE, None), P(TM, SPACE, None)),
        check_vma=False,
    )
```

time: 212 us -> 98.1 us (0.46)
  the two profiles are of different devices: /device:TPU:94 before, /device:TPU:1 now
where the time goes in v1:
time: 98.1 us; the launch traced here: 97.8 us
  Pallas kernels  54.3 us (55%)
  blocking collectives  26.3 us (27%)
  starting transfers between devices  12.8 us (13%)
  waiting for transfers between devices  1.93 us (2%)
    pallas_call x1, Pallas kernels, both_iterations(): pl.pallas_call(main_kernel, out_shape=f32(SLICES, 8, LANES), in_specs=[sm...  50.2 us
    all_to_all x1, blocking collectives, on_device(): received = lax.all_to_all(message, TM, 0, 0, tiled=True)  26.3 us
    ppermute x2, starting transfers between devices, from_offset(): lax.ppermute(array, SPACE, [((i + offset) % count, i) for i in range(coun...  9.77 us
    ppermute x1, starting transfers between devices, on_device(): far = lax.ppermute(edge, ('c', *SPACE), hops)  2.98 us
    pallas_call x1, Pallas kernels, windows(): pl.pallas_call(window_kernel, out_shape=[f32(4, ROWS, LANES), f32(4, 16,...  2.42 us
  transfers between devices with their start and end apart: 3, of which 2 were waited for; matrix products, arithmetic and copies ran while one was open for 0% of the time, Pallas kernels for 0%

profile of v1, /device:TPU:1, one launch (start us, length us, event | category | flops | bytes accessed | tf_op | source)
XLA Modules:
  0.0 97.8 jit_solution(3204911142961265583)
XLA Ops:
  0.7 0.7 pad_add_fusion.place
  1.4 2.4 %windows.1 = (f32[4,24,128]{2,1,0:T(8,128)}, f32[4,16,128]{2,1,0:T(8,128)}) custom-call(s32[4]{0:T(128)} %pad_add_fusion.place, f32[24,512]{1,0:T(8,128)} %refs_1_.1, f32[24,512]{1,0:T(8,128)} %refs_1_.1, f32[24,512]{1,0:T(8,128)} %refs_3_.1, f32[24,512]{1,0:T(8,128)} %refs_3_.1, f32[24,512]{1,0:T(8,128)} %refs_5_.1, f32[24,512]{1,0:T(8,128)} %refs_5_.1, ...), custom_call_target="tpu_custom_call" | custom-call | tf_op jit(solution)/shard_map/windows/pallas_call | solution.py:266
  3.8 0.0 copy-start.1
  3.8 7.9 %collective-permute-start.1 = (f32[4,24,128]{2,1,0:T(8,128)}, f32[4,24,128]{2,1,0:T(8,128)S(1)}, u32[]{:S(2)}, u32[]{:S(2)}) collective-permute-start(f32[4,24,128]{2,1,0:T(8,128)} %get-tuple-element.4.own), channel_id=1, source_target_pairs={{1,0},{2,1},{3,2},{4,3},{5,4},{6,5},{7,6},{8,7},{9,8},{10,9},{11,1... | collective-permute-start | bytes 147464 | tf_op jit(solution)/shard_map/ppermute | solution.py:321
  11.6 1.9 %collective-permute-start = (f32[4,24,128]{2,1,0:T(8,128)}, f32[4,24,128]{2,1,0:T(8,128)S(1)}, u32[]{:S(2)}, u32[]{:S(2)}) collective-permute-start(f32[4,24,128]{2,1,0:T(8,128)} %get-tuple-element.4.own), channel_id=1, source_target_pairs={{15,0},{0,1},{1,2},{2,3},{3,4},{4,5},{5,6},{6,7},{7,8},{8,9},{9,10... | collective-permute-start | bytes 147464 | tf_op jit(solution)/shard_map/ppermute | solution.py:321
  13.6 3.0 %collective-permute-start.2 = (f32[4,16,128]{2,1,0:T(8,128)}, f32[4,16,128]{2,1,0:T(8,128)S(1)}, u32[]{:S(2)}, u32[]{:S(2)}) collective-permute-start(f32[4,16,128]{2,1,0:T(8,128)} %get-tuple-element.5), channel_id=1, source_target_pairs={{14,0},{18,16},{15,1},{19,17},{0,2},{20,18},{1,3},{21,19},{2,4},{2... | collective-permute-start | bytes 98312 | tf_op jit(solution)/shard_map/ppermute | solution.py:340
  16.6 0.0 copy-done.1
  16.6 0.2 convert_reduce_fusion
  16.8 0.1 select_reduce_fusion.order
  16.9 1.6 %collective-permute-done.2.far = f32[4,16,128]{2,1,0:T(8,128)S(1)} collective-permute-done((f32[4,16,128]{2,1,0:T(8,128)}, f32[4,16,128]{2,1,0:T(8,128)S(1)}, u32[]{:S(2)}, u32[]{:S(2)}) %collective-permute-start.2) | collective-permute-done | bytes 32800 | tf_op jit(solution)/shard_map/ppermute | solution.py:340
  18.4 0.0 collective-permute-done.1.high
  18.4 0.4 collective-permute-done.low
  18.8 0.0 copy-start
  18.8 0.8 copy-done
  19.6 50.2 %both_iterations.1 = f32[32,8,128]{2,1,0:T(8,128)S(1)} custom-call(s32[32]{0:T(128)S(1)} %select_reduce_fusion.order, s32[32]{0:T(128)S(1)} %copy-done.1, s32[1]{0:T(128)} %bitcast.core, f32[4,24,128]{2,1,0:T(8,128)S(1)} %copy-done, f32[4,24,128]{2,1,0:T(8,128)S(1)} %collective-permute-done.low, f32[4,24,128]{2,1,0:T(8,128)S(1)} %collective-permute-done.1.high, ...), custom_call_target="tpu_custom_call" | custom-call | tf_op jit(solution)/shard_map/both_iterations/pallas_call | solution.py:298
  69.8 26.3 %all_to_all.5.received = f32[32,8,128]{2,1,0:T(8,128)} all-to-all(f32[32,8,128]{2,1,0:T(8,128)S(1)} %both_iterations.1), channel_id=1, replica_groups=mesh['zh'=4,'x'=4,'c'=2,'y'=8,'zl'=2] {'zh','x','c'}, dimensions={0} | all-to-all | bytes 262144 | tf_op jit(solution)/shard_map/all_to_all | solution.py:346
  96.1 1.7 %gathered.1 = (f32[1,24,512]{2,1,0:T(8,128)}, f32[1,24,512]{2,1,0:T(8,128)}) custom-call(f32[32,8,128]{2,1,0:T(8,128)} %all_to_all.5.received), custom_call_target="tpu_custom_call" | custom-call | tf_op jit(solution)/shard_map/gathered/pallas_call | solution.py:310
Async XLA Ops:
  3.8 12.8 %copy-start.1 = (s32[32]{0:T(128)S(1)}, s32[32]{0:T(128)}, u32[]{:S(2)}) copy-start(s32[32]{0:T(128)} %steps.1) | copy-start | bytes 388
  3.8 14.7 %collective-permute-start.1 = (f32[4,24,128]{2,1,0:T(8,128)}, f32[4,24,128]{2,1,0:T(8,128)S(1)}, u32[]{:S(2)}, u32[]{:S(2)}) collective-permute-start(f32[4,24,128]{2,1,0:T(8,128)} %get-tuple-element.4.own), channel_id=1, source_target_pairs={{1,0},{2,1},{3,2},{4,3},{5,4},{6,5},{7,6},{8,7},{9,8},{10,9},{11,1... | collective-permute-start | bytes 147464 | tf_op jit(solution)/shard_map/ppermute | solution.py:321
  11.6 7.2 %collective-permute-start = (f32[4,24,128]{2,1,0:T(8,128)}, f32[4,24,128]{2,1,0:T(8,128)S(1)}, u32[]{:S(2)}, u32[]{:S(2)}) collective-permute-start(f32[4,24,128]{2,1,0:T(8,128)} %get-tuple-element.4.own), channel_id=1, source_target_pairs={{15,0},{0,1},{1,2},{2,3},{3,4},{4,5},{5,6},{6,7},{7,8},{8,9},{9,10... | collective-permute-start | bytes 147464 | tf_op jit(solution)/shard_map/ppermute | solution.py:321
  13.6 4.9 %collective-permute-start.2 = (f32[4,16,128]{2,1,0:T(8,128)}, f32[4,16,128]{2,1,0:T(8,128)S(1)}, u32[]{:S(2)}, u32[]{:S(2)}) collective-permute-start(f32[4,16,128]{2,1,0:T(8,128)} %get-tuple-element.5), channel_id=1, source_target_pairs={{14,0},{18,16},{15,1},{19,17},{0,2},{20,18},{1,3},{21,19},{2,4},{2... | collective-permute-start | bytes 98312 | tf_op jit(solution)/shard_map/ppermute | solution.py:340
  18.8 0.8 copy-start

commit v2 on v1

--- a/solution.py
+++ b/solution.py
@@ -11,6 +11,7 @@
 SLICES = 32
 LEAST = 4
 KINDS = K - LEAST + 1
+GROUP = 8
 TM = ("zh", "x", "c")
 SPACE = ("y", "zl")
 
@@ -64,75 +65,84 @@
     return slopes, sums
 
 
-def fine_pairs(order, steps, values, densities, cost, sources, across, along, out_value, out_density, spots):
+def fine_groups(order, steps, values, densities, cost, sources, across, along, value_now, density_now, out_value, out_density, spots):
     (value_at, value_n), (density_at, density_n) = spots
-
-    def pair(number, carry):
-        own = [order[2 * number], order[2 * number + 1]]
-        trips = [steps[own[0]], steps[own[1]]]
-        most = jnp.maximum(trips[0], trips[1])
-        start = []
-        for h in range(2):
-            start.append(planes_of(values, (own[h],), value_at, value_n))
+    keep_all, share_all = 1.0 - 4.0 * time_step * diffusion, time_step * diffusion
+
+    def group(number, carry):
+        own = [order[GROUP * number + h] for h in range(GROUP)]
+        trips = [steps[j] for j in own]
+        most = trips[-1]
+        for h in range(GROUP):
+            start = planes_of(values, (own[h],), value_at, value_n)
             held = planes_of(densities, (own[h],), value_at, value_n)
             for k in range(value_n):
+                value_now[0][h, k] = value_now[1][h, k] = start[k]
                 sources[h, k] = cost[k] + (0.5 / SCALE * coupling) * held[k]
-
-        def put_slopes(h, q, slopes):
+            for k, plane in enumerate(planes_of(densities, (own[h],), density_at, density_n)):
+                density_now[0][h, k] = plane
+
+        def slopes_of(q, h):
+            now = [value_now[q % 2][h, k] for k in range(value_n)]
+            slopes, sums = slope_planes(now)
             put_planes(across, (h, q), value_at, [a for a, _ in slopes])
             put_planes(along, (h, q), value_at, [b for _, b in slopes])
-
-        def value_step(q, now):
-            result = []
-            for h in range(2):
-                active = q >= most - trips[h]
-                keep = jnp.where(active, 1.0 - 4.0 * time_step * diffusion, 1.0)
-                share = jnp.where(active, time_step * diffusion, 0.0)
-                slopes, sums = slope_planes(now[h])
-                put_slopes(h, q, slopes)
-                result.append([
-                    keep * plane + share * (sums[k] + (sources[h, k] - (slopes[k][0] * slopes[k][0] + slopes[k][1] * slopes[k][1])))
-                    for k, plane in enumerate(now[h])
-                ])
-            return result
-
-        now = lax.fori_loop(0, most, value_step, start)
-        for h in range(2):
-            put_slopes(h, most, slope_planes(now[h])[0])
-            put_planes(out_value, (own[h],), value_at, now[h])
-
-        def density_step(i, held):
-            q = most - i
-            result = []
-            for h in range(2):
-                active = i < trips[h]
-                keep = jnp.where(active, 1.0 - 4.0 * time_step * diffusion, 1.0)
-                share = jnp.where(active, time_step * diffusion, 0.0)
-                a = planes_of(across, (h, q), density_at, density_n)
-                b = planes_of(along, (h, q), density_at, density_n)
-                here = held[h]
+            return now, slopes, sums
+
+        def value_step(q):
+            for h in range(GROUP):
+                keep, share = keep_all, share_all
+                if q < K - LEAST:
+                    active = q >= K - trips[h]
+                    keep, share = jnp.where(active, keep, 1.0), jnp.where(active, share, 0.0)
+                now, slopes, sums = slopes_of(q, h)
+                for k in range(value_n):
+                    a, b = slopes[k]
+                    value_now[1 - q % 2][h, k] = keep * now[k] + share * (sums[k] + (sources[h, k] - (a * a + b * b)))
+
+        def density_step(i):
+            for h in range(GROUP):
+                keep, share = keep_all, share_all
+                if i >= LEAST:
+                    active = i < trips[h]
+                    keep, share = jnp.where(active, keep, 1.0), jnp.where(active, share, 0.0)
+                a = planes_of(across, (h, K - i), density_at, density_n)
+                b = planes_of(along, (h, K - i), density_at, density_n)
+                here = [density_now[i % 2][h, k] for k in range(density_n)]
                 twice = [plane + plane for plane in here]
                 flux = [twice[k] * a[k] for k in range(density_n)]
                 below = row_below([here[k] + flux[k] for k in range(density_n)])
                 above = row_above([here[k] - flux[k] for k in range(density_n)])
-                new = []
                 for k in range(density_n):
                     drift = twice[k] * b[k]
                     around = (below[k] + above[k]) + (right(here[k] + drift) + left(here[k] - drift))
-                    new.append(keep * here[k] + share * around)
-                result.append(new)
-            return result
-
-        begin = [planes_of(densities, (own[h],), density_at, density_n) for h in range(2)]
-        end = lax.fori_loop(0, most, density_step, begin)
-        for h in range(2):
-            put_planes(out_density, (own[h],), density_at, end[h])
+                    density_now[1 - i % 2][h, k] = keep * here[k] + share * around
+
+        for q in range(K):
+            if q < K - LEAST:
+                pl.when(q >= K - most)(lambda q=q: value_step(q))
+            else:
+                value_step(q)
+        for h in range(GROUP):
+            put_planes(out_value, (own[h],), value_at, slopes_of(K, h)[0])
+        for i in range(K):
+            if i >= LEAST:
+                pl.when(i < most)(lambda i=i: density_step(i))
+            else:
+                density_step(i)
+        for parity in range(2):
+
+            @pl.when(most % 2 == parity)
+            def _(parity=parity):
+                for h in range(GROUP):
+                    put_planes(out_density, (own[h],), density_at, [density_now[parity][h, k] for k in range(density_n)])
+
         return carry
 
-    lax.fori_loop(0, SLICES // 2, pair, 0)
-
-
-def main_kernel(order, steps, core, own, low, high, far, message, field, factors, reliefs, cost, m0, u0, m1, u1, fm, fu, across, along, sources):
+    lax.fori_loop(0, SLICES // GROUP, group, 0)
+
+
+def main_kernel(order, steps, core, own, low, high, far, message, field, factors, reliefs, cost, m0, u0, m1, u1, fm, fu, across, along, sources, va, vb, da, db):
     for part in range(4):
 
         @pl.when(core[0] == 0)
@@ -167,7 +177,7 @@
 
     lax.fori_loop(0, SLICES, opening, (field[0], field[1] * (1.0 / SCALE)))
 
-    fine_pairs(order, steps, u0, m0, planes_of(cost, (), 6, 10), sources, across, along, fu, fm, ((6, 10), (14, 8)))
+    fine_groups(order, steps, u0, m0, planes_of(cost, (), 6, 10), sources, across, along, (va, vb), (da, db), fu, fm, ((6, 10), (14, 8)))
 
     inner = pl.ds(16, FRAME2)
 
@@ -182,7 +192,7 @@
 
     lax.fori_loop(0, SLICES, first_sweep, (field[0, inner], field[1, inner] * (1.0 / SCALE)))
 
-    fine_pairs(order, steps, u1, m1, planes_of(cost, (), 22, 6), sources, across, along, fu, fm, ((6, 6), (16, 4)))
+    fine_groups(order, steps, u1, m1, planes_of(cost, (), 22, 6), sources, across, along, (va, vb), (da, db), fu, fm, ((6, 6), (16, 4)))
 
     tile, wide = pl.ds(24, 16), pl.ds(40, 16)
     lane = lax.broadcasted_iota(jnp.int32, (8, LANES), 1)
@@ -291,9 +301,13 @@
         (SLICES, FRAME2, LANES),
         (SLICES, FRAME1, LANES),
         (SLICES, FRAME1, LANES),
-        (2, K + 1, FRAME1, LANES),
-        (2, K + 1, FRAME1, LANES),
-        (2, 10, 8, LANES),
+        (GROUP, K + 1, FRAME1, LANES),
+        (GROUP, K + 1, FRAME1, LANES),
+        (GROUP, 10, 8, LANES),
+        (GROUP, 10, 8, LANES),
+        (GROUP, 10, 8, LANES),
+        (GROUP, 10, 8, LANES),
+        (GROUP, 10, 8, LANES),
     ]
     return pl.pallas_call(
         main_kernel,

time: 98.1 us -> 73.2 us (0.75)
  Pallas kernels: 54.3 us -> 29.4 us
    pallas_call x1, Pallas kernels: 50.2 us -> 25.3 us  [both_iterations(): pl.pallas_call(main_kernel, out_shape=f32(SLICES, 8, LANES), in_specs=[sm...]
where the time goes in v2:
time: 73.2 us; the launch traced here: 72.9 us
  Pallas kernels  29.4 us (40%)
  blocking collectives  26.3 us (36%)
  starting transfers between devices  12.8 us (17%)
  waiting for transfers between devices  1.93 us (3%)
  other arithmetic  0.95 us (1%)
  local copies, waits for them, and re-layouts  0.8 us (1%)
  between operations  0.76 us (1%)
    all_to_all x1, blocking collectives, on_device(): received = lax.all_to_all(message, TM, 0, 0, tiled=True)  26.3 us
    pallas_call x1, Pallas kernels, both_iterations(): pl.pallas_call(main_kernel, out_shape=f32(SLICES, 8, LANES), in_specs=[sm...  25.3 us
    ppermute x2, starting transfers between devices, from_offset(): lax.ppermute(array, SPACE, [((i + offset) % count, i) for i in range(coun...  9.77 us
    ppermute x1, starting transfers between devices, on_device(): far = lax.ppermute(edge, ('c', *SPACE), hops)  2.98 us
    pallas_call x1, Pallas kernels, windows(): pl.pallas_call(window_kernel, out_shape=[f32(4, ROWS, LANES), f32(4, 16,...  2.42 us
    pallas_call x1, Pallas kernels, gathered(): pl.pallas_call(gather_kernel, out_shape=[f32(1, ROWS, 512), f32(1, ROWS,...  1.71 us
    ppermute x1, waiting for transfers between devices, on_device(): far = lax.ppermute(edge, ('c', *SPACE), hops)  1.58 us
  transfers between devices with their start and end apart: 3, of which 2 were waited for; matrix products, arithmetic and copies ran while one was open for 0% of the time, Pallas kernels for 0%

profile of v2, /device:TPU:1, one launch (start us, length us, event | category | flops | bytes accessed | tf_op | source)
XLA Modules:
  0.0 72.9 jit_solution(11740553083520081764)
XLA Ops:
  0.7 0.7 pad_add_fusion.place
  1.4 2.4 %windows.1 = (f32[4,24,128]{2,1,0:T(8,128)}, f32[4,16,128]{2,1,0:T(8,128)}) custom-call(s32[4]{0:T(128)} %pad_add_fusion.place, f32[24,512]{1,0:T(8,128)} %refs_1_.1, f32[24,512]{1,0:T(8,128)} %refs_1_.1, f32[24,512]{1,0:T(8,128)} %refs_3_.1, f32[24,512]{1,0:T(8,128)} %refs_3_.1, f32[24,512]{1,0:T(8,128)} %refs_5_.1, f32[24,512]{1,0:T(8,128)} %refs_5_.1, ...), custom_call_target="tpu_custom_call" | custom-call | tf_op jit(solution)/shard_map/windows/pallas_call | solution.py:276
  3.8 0.0 copy-start.1
  3.8 7.9 %collective-permute-start.1 = (f32[4,24,128]{2,1,0:T(8,128)}, f32[4,24,128]{2,1,0:T(8,128)S(1)}, u32[]{:S(2)}, u32[]{:S(2)}) collective-permute-start(f32[4,24,128]{2,1,0:T(8,128)} %get-tuple-element.4.own), channel_id=1, source_target_pairs={{1,0},{2,1},{3,2},{4,3},{5,4},{6,5},{7,6},{8,7},{9,8},{10,9},{11,1... | collective-permute-start | bytes 147464 | tf_op jit(solution)/shard_map/ppermute | solution.py:335
  11.6 1.9 %collective-permute-start = (f32[4,24,128]{2,1,0:T(8,128)}, f32[4,24,128]{2,1,0:T(8,128)S(1)}, u32[]{:S(2)}, u32[]{:S(2)}) collective-permute-start(f32[4,24,128]{2,1,0:T(8,128)} %get-tuple-element.4.own), channel_id=1, source_target_pairs={{15,0},{0,1},{1,2},{2,3},{3,4},{4,5},{5,6},{6,7},{7,8},{8,9},{9,10... | collective-permute-start | bytes 147464 | tf_op jit(solution)/shard_map/ppermute | solution.py:335
  13.6 3.0 %collective-permute-start.2 = (f32[4,16,128]{2,1,0:T(8,128)}, f32[4,16,128]{2,1,0:T(8,128)S(1)}, u32[]{:S(2)}, u32[]{:S(2)}) collective-permute-start(f32[4,16,128]{2,1,0:T(8,128)} %get-tuple-element.5), channel_id=1, source_target_pairs={{14,0},{18,16},{15,1},{19,17},{0,2},{20,18},{1,3},{21,19},{2,4},{2... | collective-permute-start | bytes 98312 | tf_op jit(solution)/shard_map/ppermute | solution.py:354
  16.6 0.0 copy-done.1
  16.6 0.2 convert_reduce_fusion
  16.8 0.1 select_reduce_fusion.order
  16.9 1.6 %collective-permute-done.2.far = f32[4,16,128]{2,1,0:T(8,128)S(1)} collective-permute-done((f32[4,16,128]{2,1,0:T(8,128)}, f32[4,16,128]{2,1,0:T(8,128)S(1)}, u32[]{:S(2)}, u32[]{:S(2)}) %collective-permute-start.2) | collective-permute-done | bytes 32800 | tf_op jit(solution)/shard_map/ppermute | solution.py:354
  18.4 0.0 collective-permute-done.1.high
  18.4 0.4 collective-permute-done.low
  18.8 0.0 copy-start
  18.8 0.8 %copy-done = f32[4,24,128]{2,1,0:T(8,128)S(1)} copy-done((f32[4,24,128]{2,1,0:T(8,128)S(1)}, f32[4,24,128]{2,1,0:T(8,128)}, u32[]{:S(2)}) %copy-start) | copy-done | bytes 49176
  19.6 25.3 %both_iterations.1 = f32[32,8,128]{2,1,0:T(8,128)S(1)} custom-call(s32[32]{0:T(128)S(1)} %select_reduce_fusion.order, s32[32]{0:T(128)S(1)} %copy-done.1, s32[1]{0:T(128)} %bitcast.core, f32[4,24,128]{2,1,0:T(8,128)S(1)} %copy-done, f32[4,24,128]{2,1,0:T(8,128)S(1)} %collective-permute-done.low, f32[4,24,128]{2,1,0:T(8,128)S(1)} %collective-permute-done.1.high, ...), custom_call_target="tpu_custom_call" | custom-call | tf_op jit(solution)/shard_map/both_iterations/pallas_call | solution.py:312
  44.9 26.3 %all_to_all.5.received = f32[32,8,128]{2,1,0:T(8,128)} all-to-all(f32[32,8,128]{2,1,0:T(8,128)S(1)} %both_iterations.1), channel_id=1, replica_groups=mesh['zh'=4,'x'=4,'c'=2,'y'=8,'zl'=2] {'zh','x','c'}, dimensions={0} | all-to-all | bytes 262144 | tf_op jit(solution)/shard_map/all_to_all | solution.py:360
  71.2 1.7 %gathered.1 = (f32[1,24,512]{2,1,0:T(8,128)}, f32[1,24,512]{2,1,0:T(8,128)}) custom-call(f32[32,8,128]{2,1,0:T(8,128)} %all_to_all.5.received), custom_call_target="tpu_custom_call" | custom-call | tf_op jit(solution)/shard_map/gathered/pallas_call | solution.py:324
Async XLA Ops:
  3.8 12.8 %copy-start.1 = (s32[32]{0:T(128)S(1)}, s32[32]{0:T(128)}, u32[]{:S(2)}) copy-start(s32[32]{0:T(128)} %steps.1) | copy-start | bytes 388
  3.8 14.7 %collective-permute-start.1 = (f32[4,24,128]{2,1,0:T(8,128)}, f32[4,24,128]{2,1,0:T(8,128)S(1)}, u32[]{:S(2)}, u32[]{:S(2)}) collective-permute-start(f32[4,24,128]{2,1,0:T(8,128)} %get-tuple-element.4.own), channel_id=1, source_target_pairs={{1,0},{2,1},{3,2},{4,3},{5,4},{6,5},{7,6},{8,7},{9,8},{10,9},{11,1... | collective-permute-start | bytes 147464 | tf_op jit(solution)/shard_map/ppermute | solution.py:335
  11.6 7.2 %collective-permute-start = (f32[4,24,128]{2,1,0:T(8,128)}, f32[4,24,128]{2,1,0:T(8,128)S(1)}, u32[]{:S(2)}, u32[]{:S(2)}) collective-permute-start(f32[4,24,128]{2,1,0:T(8,128)} %get-tuple-element.4.own), channel_id=1, source_target_pairs={{15,0},{0,1},{1,2},{2,3},{3,4},{4,5},{5,6},{6,7},{7,8},{8,9},{9,10... | collective-permute-start | bytes 147464 | tf_op jit(solution)/shard_map/ppermute | solution.py:335
  13.6 4.9 %collective-permute-start.2 = (f32[4,16,128]{2,1,0:T(8,128)}, f32[4,16,128]{2,1,0:T(8,128)S(1)}, u32[]{:S(2)}, u32[]{:S(2)}) collective-permute-start(f32[4,16,128]{2,1,0:T(8,128)} %get-tuple-element.5), channel_id=1, source_target_pairs={{14,0},{18,16},{15,1},{19,17},{0,2},{20,18},{1,3},{21,19},{2,4},{2... | collective-permute-start | bytes 98312 | tf_op jit(solution)/shard_map/ppermute | solution.py:354
  18.8 0.8 %copy-start = (f32[4,24,128]{2,1,0:T(8,128)S(1)}, f32[4,24,128]{2,1,0:T(8,128)}, u32[]{:S(2)}) copy-start(f32[4,24,128]{2,1,0:T(8,128)} %get-tuple-element.4.own) | copy-start | bytes 147460

commit v3 on v2

v3 whole, which is shorter than its diff:
```python
import jax
import jax.numpy as jnp
from jax import lax
from jax.experimental import pallas as pl
from jax.experimental.pallas import tpu as pltpu
from jax.sharding import Mesh
from jax.sharding import PartitionSpec as P


K = 8
SLICES = 32
LEAST = 4
KINDS = K - LEAST + 1
GROUP = 8
TM = ("zh", "x", "c")
SPACE = ("y", "zl")

time_step = 0.05
diffusion = 2.0
coupling = 0.1

ROWS = 24
TILE_ROWS = 6
TILE_COLS = 64
LANES = 128
COL_AT = 32
FRAME1 = 80
FRAME2 = 48
TOP = 7
PARTS = 5
EDGED = (1, 2, 3)
SCALE = 16.0


def planes_of(ref, at, start, count):
    return [ref[(*at, pl.ds(start + k, 8, stride=count), slice(None))] for k in range(count)]


def put_planes(ref, at, start, planes):
    count = len(planes)
    for k, plane in enumerate(planes):
        ref[(*at, pl.ds(start + k, 8, stride=count), slice(None))] = plane


def row_above(planes):
    return [pltpu.roll(planes[-1], 1, 0), *planes[:-1]]


def row_below(planes):
    return [*planes[1:], pltpu.roll(planes[0], 7, 0)]


def left(plane):
    return pltpu.roll(plane, 1, 1)


def right(plane):
    return pltpu.roll(plane, LANES - 1, 1)


def lanes_of(shape):
    return lax.broadcasted_iota(jnp.int32, shape, len(shape) - 1)


def slope_planes(planes, beside=None):
    up, down = row_above(planes), row_below(planes)
    slopes, sums = [], []
    for k, plane in enumerate(planes):
        west, east = left(plane), right(plane)
        if beside is not None:
            lane = lanes_of(plane.shape)
            west, east = jnp.where(lane == 0, beside[k], west), jnp.where(lane == LANES - 1, beside[k], east)
        slopes.append((down[k] - up[k], east - west))
        sums.append((up[k] + down[k]) + (west + east))
    return slopes, sums


def fine_groups(table, values, beside, densities, cost, sources, across, along, value_now, density_now, out_value, out_density, spots):
    (value_at, value_n), (density_at, density_n) = spots
    keep_all, share_all = 1.0 - 4.0 * time_step * diffusion, time_step * diffusion

    def group(number, carry):
        own = [table[GROUP * number + h] for h in range(GROUP)]
        trips = [table[SLICES + j] for j in own]
        most = trips[-1]
        for h in range(GROUP):
            start = planes_of(values, (own[h],), value_at, value_n)
            held = planes_of(densities, (own[h],), value_at, value_n)
            for k in range(value_n):
                value_now[0][h, k] = value_now[1][h, k] = start[k]
                sources[h, k] = cost[k] + (0.5 / SCALE * coupling) * held[k]
            for k, plane in enumerate(planes_of(densities, (own[h],), density_at, density_n)):
                density_now[0][h, k] = plane

        def slopes_of(q, h):
            now = [value_now[q % 2][h, k] for k in range(value_n)]
            edges = planes_of(beside, (own[h],), value_at, value_n) if q == 0 and beside is not None else None
            slopes, sums = slope_planes(now, edges)
            put_planes(across, (h, q), value_at, [a for a, _ in slopes])
            put_planes(along, (h, q), value_at, [b for _, b in slopes])
            return now, slopes, sums

        def value_step(q):
            for h in range(GROUP):
                keep, share = keep_all, share_all
                if q < K - LEAST:
                    active = q >= K - trips[h]
                    keep, share = jnp.where(active, keep, 1.0), jnp.where(active, share, 0.0)
                now, slopes, sums = slopes_of(q, h)
                for k in range(value_n):
                    a, b = slopes[k]
                    value_now[1 - q % 2][h, k] = keep * now[k] + share * (sums[k] + (sources[h, k] - (a * a + b * b)))

        def density_step(i):
            for h in range(GROUP):
                keep, share = keep_all, share_all
                if i >= LEAST:
                    active = i < trips[h]
                    keep, share = jnp.where(active, keep, 1.0), jnp.where(active, share, 0.0)
                a = planes_of(across, (h, K - i), density_at, density_n)
                b = planes_of(along, (h, K - i), density_at, density_n)
                here = [density_now[i % 2][h, k] for k in range(density_n)]
                twice = [plane + plane for plane in here]
                flux = [twice[k] * a[k] for k in range(density_n)]
                below = row_below([here[k] + flux[k] for k in range(density_n)])
                above = row_above([here[k] - flux[k] for k in range(density_n)])
                for k in range(density_n):
                    drift = twice[k] * b[k]
                    around = (below[k] + above[k]) + (right(here[k] + drift) + left(here[k] - drift))
                    density_now[1 - i % 2][h, k] = keep * here[k] + share * around

        for q in range(K):
            if q < K - LEAST:
                pl.when(q >= K - most)(lambda q=q: value_step(q))
            else:
                value_step(q)
        for h in range(GROUP):
            put_planes(out_value, (own[h],), value_at, slopes_of(K, h)[0])
        for i in range(K):
            if i >= LEAST:
                pl.when(i < most)(lambda i=i: density_step(i))
            else:
                density_step(i)
        for parity in range(2):

            @pl.when(most % 2 == parity)
            def _(parity=parity):
                for h in range(GROUP):
                    put_planes(out_density, (own[h],), density_at, [density_now[parity][h, k] for k in range(density_n)])

        return carry

    lax.fori_loop(0, SLICES // GROUP, group, 0)


def main_kernel(table, own, near, far, message, field, factors, reliefs, cost, m0, u0, e0, m1, u1, fm, fu, across, along, sources, va, vb, da, db):
    band, half = table[2 * SLICES], table[2 * SLICES + 1]
    for position in range(4):

        @pl.when(band == position)
        def _(position=position):
            pieces = [(near, (0,), ROWS, -24), (own, (), ROWS, 0), (near, (1,), ROWS, 24), (far, (), 16, -40 if position < 2 else 48)]
            for ref, at, rows, first in pieces:
                begin = first - TILE_ROWS * position + 40
                low, high = max(begin, TOP), min(begin + rows, FRAME1 - 1)
                for part in range(PARTS):
                    field[part, low:high] = ref[(*at, part, slice(low - begin, high - begin))]

    packed_edges = field[4]
    lane = lanes_of((FRAME1, LANES))
    edges = {}
    for place, part in enumerate(EDGED):
        edges[part] = jnp.where(lane < 64, pltpu.roll(packed_edges, (LANES - place) % LANES, 1), pltpu.roll(packed_edges, place, 1)) if place else packed_edges
    for begin, rate, running in ((0, field[3], field[2]), (KINDS, edges[3], edges[2])):
        quotient = running / rate
        for kind in range(KINDS):
            factor = jnp.exp(rate * (-time_step * (LEAST + kind)))
            factors[begin + kind] = factor
            reliefs[begin + kind] = (1.0 - factor) * quotient * (1.0 / SCALE)
    cost[...] = field[2] * (0.5 / SCALE)

    def opening(j, now):
        density, value, edge = now
        back = SLICES - 1 - j
        m0[j] = density
        u0[back] = value
        e0[back] = edge
        kind = table[SLICES + back] - LEAST
        density = factors[table[SLICES + j] - LEAST] * density
        value = factors[kind] * value + reliefs[kind]
        edge = factors[KINDS + kind] * edge + reliefs[KINDS + kind]
        return density, value, edge

    lax.fori_loop(0, SLICES, opening, (field[0], field[1] * (1.0 / SCALE), edges[1] * (1.0 / SCALE)))

    fine_groups(table, u0, e0, m0, planes_of(cost, (), 7, 9), sources, across, along, (va, vb), (da, db), fu, fm, ((7, 9), (15, 7)))

    inner = pl.ds(16, FRAME2)

    def first_sweep(j, now):
        density, value = now
        back = SLICES - 1 - j
        m1[j] = density
        u1[back] = value
        density = factors[table[SLICES + j] - LEAST, inner] * (density - m0[j, inner]) + fm[j, inner]
        value = factors[table[SLICES + back] - LEAST, inner] * (value - u0[back, inner]) + fu[back, inner]
        return density, value

    lax.fori_loop(0, SLICES, first_sweep, (field[0, inner], field[1, inner] * (1.0 / SCALE)))

    fine_groups(table, u1, None, m1, planes_of(cost, (), 23, 5), sources, across, along, (va, vb), (da, db), fu, fm, ((7, 5), (15, 3)))

    tile, wide = pl.ds(24, 8), pl.ds(40, 8)

    def second_sweep(j, now):
        density, value = now
        back = SLICES - 1 - j
        u0[back, 0:8] = value
        m0[j, 0:8] = density
        density = factors[table[SLICES + j] - LEAST, wide] * (density - m1[j, tile]) + fm[j, tile]
        value = factors[table[SLICES + back] - LEAST, wide] * (value - u1[back, tile]) + fu[back, tile]
        return density, value

    lax.fori_loop(0, SLICES, second_sweep, (field[0, wide], field[1, wide] * (1.0 / SCALE)))

    first_half = lanes_of((8, LANES)) < 64
    for j in range(SLICES):
        density, value = m0[j, 0:8], SCALE * u0[j, 0:8]
        ahead, behind = jnp.where(half == 0, density, value), jnp.where(half == 0, value, density)
        message[j] = jnp.where(first_half, pltpu.roll(ahead, LANES - COL_AT, 1), pltpu.roll(behind, COL_AT, 1))


def place_of():
    zh, x, c = (lax.axis_index(axis) for axis in TM)
    return 2 * c + x % 2, 2 * zh + x // 2, x // 2, c


def window_kernel(*refs):
    arrays, (near, far), (blocks, arrived) = refs[:4], refs[4:6], refs[6:]
    _, column, _, core = place_of()
    begin = (column * TILE_COLS + 512 - COL_AT) % 512
    first, shift = begin // LANES, LANES - begin % LANES
    copies = []
    for part, array in enumerate(arrays):
        for which in range(2):
            at = pl.multiple_of(((first + which) % 4) * LANES, LANES)
            copies.append(pltpu.make_async_copy(array.at[:, pl.ds(at, LANES)], blocks.at[part, which], arrived.at[part, which]))
    for copy in copies:
        copy.start()
    for copy in copies:
        copy.wait()
    lane = lanes_of((ROWS, LANES))
    beside = jnp.zeros((ROWS, LANES), jnp.float32)
    for part in range(PARTS):
        if part < 4:
            a, b = blocks[part, 0], blocks[part, 1]
            window = jnp.where(lane < shift, pltpu.roll(a, shift, 1), pltpu.roll(b, shift, 1))
        else:
            window = beside
        near[part] = window

        @pl.when(core == 0)
        def _(window=window, part=part):
            far[part] = window[8:24]

        @pl.when(core != 0)
        def _(window=window, part=part):
            far[part] = window[0:16]

        if part in EDGED:
            place = EDGED.index(part)
            beside = jnp.where(lane == place, pltpu.roll(a, shift + 1 + place, 1), beside)
            beside = jnp.where(lane == LANES - 1 - place, pltpu.roll(b, shift - 1 - place, 1), beside)


def gather_kernel(received, density, value):
    first_half = lanes_of((8, LANES)) < 64
    for zh in range(4):
        for band in range(4):
            at = [zh * 8 + (2 * half + band % 2) * 2 + band // 2 for half in range(2)]
            a, b = received[at[0]], received[at[1]]
            rows, lanes = slice(TILE_ROWS * band, TILE_ROWS * (band + 1)), slice(LANES * zh, LANES * (zh + 1))
            density[0, rows, lanes] = jnp.where(first_half, a, b)[0:TILE_ROWS]
            value[0, rows, lanes] = pltpu.roll(jnp.where(first_half, b, a), 64, 1)[0:TILE_ROWS]


def vmem():
    return pl.BlockSpec(memory_space=pltpu.VMEM)


def smem():
    return pl.BlockSpec(memory_space=pltpu.SMEM)


def f32(*shape):
    return jax.ShapeDtypeStruct(shape, jnp.float32)


def windows(*arrays):
    return pl.pallas_call(
        window_kernel,
        out_shape=[f32(PARTS, ROWS, LANES), f32(PARTS, 16, LANES)],
        in_specs=[pl.BlockSpec(memory_space=pl.ANY)] * 4,
        out_specs=[vmem(), vmem()],
        scratch_shapes=[pltpu.VMEM((4, 2, ROWS, LANES), jnp.float32), pltpu.SemaphoreType.DMA((4, 2))],
        name="windows",
    )(*arrays)


def both_iterations(table, own, near, far):
    scratch = [
        (PARTS, FRAME1, LANES),
        (2 * KINDS, FRAME1, LANES),
        (2 * KINDS, FRAME1, LANES),
        (FRAME1, LANES),
        (SLICES, FRAME1, LANES),
        (SLICES, FRAME1, LANES),
        (SLICES, FRAME1, LANES),
        (SLICES, FRAME2, LANES),
        (SLICES, FRAME2, LANES),
        (SLICES, FRAME1, LANES),
        (SLICES, FRAME1, LANES),
        (GROUP, K + 1, FRAME1, LANES),
        (GROUP, K + 1, FRAME1, LANES),
        (GROUP, 9, 8, LANES),
        (GROUP, 9, 8, LANES),
        (GROUP, 9, 8, LANES),
        (GROUP, 9, 8, LANES),
        (GROUP, 9, 8, LANES),
    ]
    return pl.pallas_call(
        main_kernel,
        out_shape=f32(SLICES, 8, LANES),
        in_specs=[smem(), vmem(), vmem(), vmem()],
        out_specs=vmem(),
        scratch_shapes=[pltpu.VMEM(shape, jnp.float32) for shape in scratch],
        compiler_params=pltpu.CompilerParams(vmem_limit_bytes=32 * 2**20),
        name="both_iterations",
    )(table, own, near, far)


def gathered(received):
    return pl.pallas_call(
        gather_kernel,
        out_shape=[f32(1, ROWS, 512), f32(1, ROWS, 512)],
        in_specs=[vmem()],
        out_specs=[vmem(), vmem()],
        name="gathered",
    )(received)


def toward_own_side(array, distance):
    hops = []
    for c in range(2):
        for space in range(16):
            source = (space + (distance if c else -distance)) % 16
            hops.append((c * 16 + source, c * 16 + space))
    return lax.ppermute(array, ("c", *SPACE), hops)


def on_device(initial_density, terminal_cost, running_cost, discount_rate, slice_steps):
    own, edge = windows(initial_density, terminal_cost, running_cost, discount_rate)
    beside = toward_own_side(own, 1)
    far = toward_own_side(edge, 2)
    near = lax.all_gather(beside, "c")
    band, _, half, _ = place_of()
    numbers = jnp.arange(SLICES, dtype=jnp.int32)
    ahead = (slice_steps[None, :] < slice_steps[:, None]) | ((slice_steps[None, :] == slice_steps[:, None]) & (numbers[None, :] < numbers[:, None]))
    rank = jnp.sum(ahead.astype(jnp.int32), axis=1)
    order = jnp.sum(jnp.where(rank[None, :] == numbers[:, None], numbers[None, :], 0), axis=1)
    table = jnp.concatenate([order, slice_steps, jnp.stack([band, half]).astype(jnp.int32)])
    message = both_iterations(table, own, near, far)
    received = lax.all_to_all(message, TM, 0, 0, tiled=True)
    return tuple(gathered(received))


def solution(mesh):
    finer = Mesh(mesh.devices.reshape(4, 4, 2, 8, 2), ("zh", "x", "c", "y", "zl"))
    placed = (P(SPACE, None), P(SPACE, None), P(SPACE, None), P(SPACE, None), P())
    return jax.shard_map(
        on_device,
        mesh=finer,
        in_specs=placed,
        out_specs=(P(TM, SPACE, None), P(TM, SPACE, None)),
        check_vma=False,
    )
```

time: 73.2 us -> 62.7 us (0.86)
  Pallas kernels: 29.4 us -> 23 us
  starting transfers between devices: 12.8 us -> 10.7 us
  waiting for transfers between devices: 1.93 us -> 0.52 us
    all_gather x0 -> x1, blocking collectives: none -> 6.46 us  [on_device(): near = lax.all_gather(beside, 'c')]
    all_to_all x1, blocking collectives: 26.3 us -> 20 us  [on_device(): received = lax.all_to_all(message, TM, 0, 0, tiled=True)]
    pallas_call x1, Pallas kernels: 25.3 us -> 19.5 us  [both_iterations(): pl.pallas_call(main_kernel, out_shape=f32(SLICES, 8, LANES), in_specs=[sm...]
    ppermute x3 -> x2, starting transfers between devices: 12.8 us -> 10.7 us  [toward_own_side(): return lax.ppermute(array, ('c', *SPACE), hops)]
    ppermute x3 -> x2, waiting for transfers between devices: 1.93 us -> 0.52 us  [toward_own_side(): return lax.ppermute(array, ('c', *SPACE), hops)]
  transfers between devices with their start and end apart: 3 -> 2, of which waited for: 2 -> 1; matrix products, arithmetic and copies ran while one was open for 0% -> 1% of each run, Pallas kernels for 0% -> 0%
where the time goes in v3:
time: 62.7 us; the launch traced here: 62.5 us
  blocking collectives  26.5 us (42%)
  Pallas kernels  23 us (37%)
  starting transfers between devices  10.7 us (17%)
  between operations  0.71 us (1%)
  local copies, waits for them, and re-layouts  0.65 us (1%)
    all_to_all x1, blocking collectives, on_device(): received = lax.all_to_all(message, TM, 0, 0, tiled=True)  20 us
    pallas_call x1, Pallas kernels, both_iterations(): pl.pallas_call(main_kernel, out_shape=f32(SLICES, 8, LANES), in_specs=[sm...  19.5 us
    ppermute x2, starting transfers between devices, toward_own_side(): return lax.ppermute(array, ('c', *SPACE), hops)  10.7 us
    all_gather x1, blocking collectives, on_device(): near = lax.all_gather(beside, 'c')  6.46 us
    pallas_call x1, Pallas kernels, windows(): pl.pallas_call(window_kernel, out_shape=[f32(PARTS, ROWS, LANES), f32(PAR...  1.95 us
    pallas_call x1, Pallas kernels, gathered(): pl.pallas_call(gather_kernel, out_shape=[f32(1, ROWS, 512), f32(1, ROWS,...  1.61 us
  transfers between devices with their start and end apart: 2, of which 1 were waited for; matrix products, arithmetic and copies ran while one was open for 1% of the time, Pallas kernels for 0%

profile of v3, /device:TPU:1, one launch (start us, length us, event | category | flops | bytes accessed | tf_op | source)
XLA Modules:
  0.0 62.5 jit_solution(3819328455700098172)
XLA Ops:
  0.6 1.9 %windows.1 = (f32[5,24,128]{2,1,0:T(8,128)}, f32[5,16,128]{2,1,0:T(8,128)}) custom-call(f32[24,512]{1,0:T(8,128)} %refs_0_.1, f32[24,512]{1,0:T(8,128)} %refs_1_.1, f32[24,512]{1,0:T(8,128)} %refs_2_.1, f32[24,512]{1,0:T(8,128)} %refs_3_.1), custom_call_target="tpu_custom_call" | custom-call | tf_op jit(solution)/shard_map/windows/pallas_call | solution.py:300
  2.6 5.9 %collective-permute-start.1 = (f32[5,16,128]{2,1,0:T(8,128)}, f32[5,16,128]{2,1,0:T(8,128)S(1)}, u32[]{:S(2)}, u32[]{:S(2)}) collective-permute-start(f32[5,16,128]{2,1,0:T(8,128)} %get-tuple-element.5), channel_id=1, source_target_pairs={{14,0},{15,1},{0,2},{1,3},{2,4},{3,5},{4,6},{5,7},{6,8},{7,9},{8,1... | collective-permute-start | bytes 122888 | tf_op jit(solution)/shard_map/ppermute | solution.py:358
  8.5 4.8 %collective-permute-start = (f32[5,24,128]{2,1,0:T(8,128)}, f32[5,24,128]{2,1,0:T(8,128)S(1)}, u32[]{:S(2)}, u32[]{:S(2)}) collective-permute-start(f32[5,24,128]{2,1,0:T(8,128)} %get-tuple-element.4.own), channel_id=1, source_target_pairs={{15,0},{0,1},{1,2},{2,3},{3,4},{4,5},{5,6},{6,7},{7,8},{8,9},{9,10... | collective-permute-start | bytes 184328 | tf_op jit(solution)/shard_map/ppermute | solution.py:358
  13.3 0.0 copy-start.1
  13.3 0.6 %copy-done.1 = s32[32]{0:T(128)S(1)} copy-done((s32[32]{0:T(128)S(1)}, s32[32]{0:T(128)}, u32[]{:S(2)}) %copy-start.1) | copy-done | bytes 152
  14.0 0.2 convert_reduce_fusion
  14.2 0.1 select_reduce_fusion
  14.3 0.1 pad_add_fusion.table
  14.4 0.0 copy-start
  14.4 0.5 collective-permute-done
  14.9 6.5 %all-gather = f32[10,24,128]{2,1,0:T(8,128)S(1)} all-gather(f32[5,24,128]{2,1,0:T(8,128)S(1)} %collective-permute-done), channel_id=2, replica_groups=mesh['zh'=4,'x'=4,'c'=2,'y'=8,'zl'=2] {'c'}, dimensions={0}, use_global_device_ids=true | all-gather | bytes 184320 | tf_op jit(solution)/shard_map/all_gather | solution.py:365
  21.4 0.0 collective-permute-done.1.far
  21.4 0.0 copy-done
  21.4 19.5 %both_iterations.1 = f32[32,8,128]{2,1,0:T(8,128)S(1)} custom-call(s32[66]{0:T(128)S(1)} %pad_add_fusion.table, f32[5,24,128]{2,1,0:T(8,128)S(1)} %copy-done, f32[2,5,24,128]{3,2,1,0:T(8,128)S(1)} %bitcast.3, f32[5,16,128]{2,1,0:T(8,128)S(1)} %collective-permute-done.1.far), custom_call_target="tpu_custom_call" | custom-call | tf_op jit(solution)/shard_map/both_iterations/pallas_call | solution.py:331
  40.8 20.0 %all_to_all.5.received = f32[32,8,128]{2,1,0:T(8,128)} all-to-all(f32[32,8,128]{2,1,0:T(8,128)S(1)} %both_iterations.1), channel_id=1, replica_groups=mesh['zh'=4,'x'=4,'c'=2,'y'=8,'zl'=2] {'zh','x','c'}, dimensions={0} | all-to-all | bytes 262144 | tf_op jit(solution)/shard_map/all_to_all | solution.py:373
  60.8 1.6 %gathered.1 = (f32[1,24,512]{2,1,0:T(8,128)}, f32[1,24,512]{2,1,0:T(8,128)}) custom-call(f32[32,8,128]{2,1,0:T(8,128)} %all_to_all.5.received), custom_call_target="tpu_custom_call" | custom-call | tf_op jit(solution)/shard_map/gathered/pallas_call | solution.py:343
Async XLA Ops:
  2.6 18.8 %collective-permute-start.1 = (f32[5,16,128]{2,1,0:T(8,128)}, f32[5,16,128]{2,1,0:T(8,128)S(1)}, u32[]{:S(2)}, u32[]{:S(2)}) collective-permute-start(f32[5,16,128]{2,1,0:T(8,128)} %get-tuple-element.5), channel_id=1, source_target_pairs={{14,0},{15,1},{0,2},{1,3},{2,4},{3,5},{4,6},{5,7},{6,8},{7,9},{8,1... | collective-permute-start | bytes 122888 | tf_op jit(solution)/shard_map/ppermute | solution.py:358
  8.5 6.4 %collective-permute-start = (f32[5,24,128]{2,1,0:T(8,128)}, f32[5,24,128]{2,1,0:T(8,128)S(1)}, u32[]{:S(2)}, u32[]{:S(2)}) collective-permute-start(f32[5,24,128]{2,1,0:T(8,128)} %get-tuple-element.4.own), channel_id=1, source_target_pairs={{15,0},{0,1},{1,2},{2,3},{3,4},{4,5},{5,6},{6,7},{7,8},{8,9},{9,10... | collective-permute-start | bytes 184328 | tf_op jit(solution)/shard_map/ppermute | solution.py:358
  13.3 0.7 %copy-start.1 = (s32[32]{0:T(128)S(1)}, s32[32]{0:T(128)}, u32[]{:S(2)}) copy-start(s32[32]{0:T(128)} %param.9) | copy-start | bytes 388
  14.4 7.0 %copy-start = (f32[5,24,128]{2,1,0:T(8,128)S(1)}, f32[5,24,128]{2,1,0:T(8,128)}, u32[]{:S(2)}) copy-start(f32[5,24,128]{2,1,0:T(8,128)} %get-tuple-element.4.own) | copy-start | bytes 184324

commit v4 on v3

--- a/solution.py
+++ b/solution.py
@@ -191,7 +191,7 @@
         edge = factors[KINDS + kind] * edge + reliefs[KINDS + kind]
         return density, value, edge
 
-    lax.fori_loop(0, SLICES, opening, (field[0], field[1] * (1.0 / SCALE), edges[1] * (1.0 / SCALE)))
+    lax.fori_loop(0, SLICES, opening, (field[0], field[1] * (1.0 / SCALE), edges[1] * (1.0 / SCALE)), unroll=2)
 
     fine_groups(table, u0, e0, m0, planes_of(cost, (), 7, 9), sources, across, along, (va, vb), (da, db), fu, fm, ((7, 9), (15, 7)))
 
@@ -206,7 +206,7 @@
         value = factors[table[SLICES + back] - LEAST, inner] * (value - u0[back, inner]) + fu[back, inner]
         return density, value
 
-    lax.fori_loop(0, SLICES, first_sweep, (field[0, inner], field[1, inner] * (1.0 / SCALE)))
+    lax.fori_loop(0, SLICES, first_sweep, (field[0, inner], field[1, inner] * (1.0 / SCALE)), unroll=4)
 
     fine_groups(table, u1, None, m1, planes_of(cost, (), 23, 5), sources, across, along, (va, vb), (da, db), fu, fm, ((7, 5), (15, 3)))
 
@@ -221,7 +221,7 @@
         value = factors[table[SLICES + back] - LEAST, wide] * (value - u1[back, tile]) + fu[back, tile]
         return density, value
 
-    lax.fori_loop(0, SLICES, second_sweep, (field[0, wide], field[1, wide] * (1.0 / SCALE)))
+    lax.fori_loop(0, SLICES, second_sweep, (field[0, wide], field[1, wide] * (1.0 / SCALE)), unroll=8)
 
     first_half = lanes_of((8, LANES)) < 64
     for j in range(SLICES):
@@ -345,6 +345,7 @@
         out_shape=[f32(1, ROWS, 512), f32(1, ROWS, 512)],
         in_specs=[vmem()],
         out_specs=[vmem(), vmem()],
+        compiler_params=pltpu.CompilerParams(vmem_limit_bytes=2 * 2**20),
         name="gathered",
     )(received)
 
@@ -361,7 +362,6 @@
 def on_device(initial_density, terminal_cost, running_cost, discount_rate, slice_steps):
     own, edge = windows(initial_density, terminal_cost, running_cost, discount_rate)
     beside = toward_own_side(own, 1)
-    far = toward_own_side(edge, 2)
     near = lax.all_gather(beside, "c")
     band, _, half, _ = place_of()
     numbers = jnp.arange(SLICES, dtype=jnp.int32)
@@ -369,6 +369,8 @@
     rank = jnp.sum(ahead.astype(jnp.int32), axis=1)
     order = jnp.sum(jnp.where(rank[None, :] == numbers[:, None], numbers[None, :], 0), axis=1)
     table = jnp.concatenate([order, slice_steps, jnp.stack([band, half]).astype(jnp.int32)])
+    edge, table = lax.optimization_barrier((edge, table))
+    far = toward_own_side(edge, 2)
     message = both_iterations(table, own, near, far)
     received = lax.all_to_all(message, TM, 0, 0, tiled=True)
     return tuple(gathered(received))

time: 62.7 us -> 58.8 us (0.938)
  Pallas kernels: 23 us -> 20.4 us
  blocking collectives: 26.5 us -> 25.4 us
    pallas_call x1, Pallas kernels: 19.5 us -> 17.8 us  [both_iterations(): pl.pallas_call(main_kernel, out_shape=f32(SLICES, 8, LANES), in_specs=[sm...]
    all_gather x1, blocking collectives: 6.46 us -> 4.91 us  [on_device(): near = lax.all_gather(beside, 'c')]
    pallas_call x1, Pallas kernels: 1.61 us -> 0.71 us  [gathered(): pl.pallas_call(gather_kernel, out_shape=[f32(1, ROWS, 512), f32(1, ROWS,...]
  transfers between devices with their start and end apart: 2 -> 2, of which waited for: 1 -> 0; matrix products, arithmetic and copies ran while one was open for 1% -> 1% of each run, Pallas kernels for 0% -> 0%
where the time goes in v4:
time: 58.8 us; the launch traced here: 58.5 us
  blocking collectives  25.4 us (43%)
  Pallas kernels  20.4 us (35%)
  starting transfers between devices  10.8 us (18%)
  between operations  0.73 us (1%)
  local copies, waits for them, and re-layouts  0.66 us (1%)
    all_to_all x1, blocking collectives, on_device(): received = lax.all_to_all(message, TM, 0, 0, tiled=True)  20.5 us
    pallas_call x1, Pallas kernels, both_iterations(): pl.pallas_call(main_kernel, out_shape=f32(SLICES, 8, LANES), in_specs=[sm...  17.8 us
    ppermute x2, starting transfers between devices, toward_own_side(): return lax.ppermute(array, ('c', *SPACE), hops)  10.8 us
    all_gather x1, blocking collectives, on_device(): near = lax.all_gather(beside, 'c')  4.91 us
    pallas_call x1, Pallas kernels, windows(): pl.pallas_call(window_kernel, out_shape=[f32(PARTS, ROWS, LANES), f32(PAR...  1.95 us
  transfers between devices with their start and end apart: 2, of which 0 were waited for; matrix products, arithmetic and copies ran while one was open for 1% of the time, Pallas kernels for 0%

profile of v4, /device:TPU:1, one launch (start us, length us, event | category | flops | bytes accessed | tf_op | source)
XLA Modules:
  0.0 58.5 jit_solution(901868130557422818)
XLA Ops:
  0.6 1.9 %windows.1 = (f32[5,24,128]{2,1,0:T(8,128)}, f32[5,16,128]{2,1,0:T(8,128)}) custom-call(f32[24,512]{1,0:T(8,128)} %refs_0_.1, f32[24,512]{1,0:T(8,128)} %refs_1_.1, f32[24,512]{1,0:T(8,128)} %refs_2_.1, f32[24,512]{1,0:T(8,128)} %refs_3_.1), custom_call_target="tpu_custom_call" | custom-call | tf_op jit(solution)/shard_map/windows/pallas_call | solution.py:300
  2.6 0.0 copy-start.2
  2.6 7.7 %collective-permute-start = (f32[5,24,128]{2,1,0:T(8,128)}, f32[5,24,128]{2,1,0:T(8,128)S(1)}, u32[]{:S(2)}, u32[]{:S(2)}) collective-permute-start(f32[5,24,128]{2,1,0:T(8,128)} %get-tuple-element.8.own), channel_id=1, source_target_pairs={{15,0},{0,1},{1,2},{2,3},{3,4},{4,5},{5,6},{6,7},{7,8},{8,9},{9,10... | collective-permute-start | bytes 184328 | tf_op jit(solution)/shard_map/ppermute | solution.py:359
  10.4 0.0 copy-start.1
  10.4 0.6 %copy-done.1 = s32[32]{0:T(128)S(1)} copy-done((s32[32]{0:T(128)S(1)}, s32[32]{0:T(128)}, u32[]{:S(2)}) %copy-start.1) | copy-done | bytes 152
  11.0 0.2 convert_reduce_fusion
  11.2 0.1 select_reduce_fusion
  11.3 0.1 pad_add_fusion.table
  11.4 0.0 copy-done.2
  11.4 0.0 copy-start
  11.4 3.1 %collective-permute-start.1 = (f32[5,16,128]{2,1,0:T(8,128)S(1)}, f32[5,16,128]{2,1,0:T(8,128)S(1)}, u32[]{:S(2)}, u32[]{:S(2)}) collective-permute-start(f32[5,16,128]{2,1,0:T(8,128)S(1)} %copy-done.2), channel_id=1, source_target_pairs={{14,0},{15,1},{0,2},{1,3},{2,4},{3,5},{4,6},{5,7},{6,8},{7,9},{8,1... | collective-permute-start | bytes 122888 | tf_op jit(solution)/shard_map/ppermute | solution.py:359
  14.5 0.0 collective-permute-done
  14.5 4.9 %all-gather = f32[10,24,128]{2,1,0:T(8,128)S(1)} all-gather(f32[5,24,128]{2,1,0:T(8,128)S(1)} %collective-permute-done), channel_id=2, replica_groups=mesh['zh'=4,'x'=4,'c'=2,'y'=8,'zl'=2] {'c'}, dimensions={0}, use_global_device_ids=true | all-gather | bytes 184320 | tf_op jit(solution)/shard_map/all_gather | solution.py:365
  19.4 0.0 collective-permute-done.1.far
  19.4 0.0 copy-done
  19.4 17.8 %both_iterations.1 = f32[32,8,128]{2,1,0:T(8,128)S(1)} custom-call(s32[66]{0:T(128)S(1)} %pad_add_fusion.table, f32[5,24,128]{2,1,0:T(8,128)S(1)} %copy-done, f32[2,5,24,128]{3,2,1,0:T(8,128)S(1)} %bitcast.3, f32[5,16,128]{2,1,0:T(8,128)S(1)} %collective-permute-done.1.far), custom_call_target="tpu_custom_call" | custom-call | tf_op jit(solution)/shard_map/both_iterations/pallas_call | solution.py:331
  37.2 20.5 %all_to_all.5.received = f32[32,8,128]{2,1,0:T(8,128)S(1)} all-to-all(f32[32,8,128]{2,1,0:T(8,128)S(1)} %both_iterations.1), channel_id=1, replica_groups=mesh['zh'=4,'x'=4,'c'=2,'y'=8,'zl'=2] {'zh','x','c'}, dimensions={0} | all-to-all | bytes 262144 | tf_op jit(solution)/shard_map/all_to_all | solution.py:375
  57.8 0.7 %gathered.1 = (f32[1,24,512]{2,1,0:T(8,128)}, f32[1,24,512]{2,1,0:T(8,128)}) custom-call(f32[32,8,128]{2,1,0:T(8,128)S(1)} %all_to_all.5.received), custom_call_target="tpu_custom_call" | custom-call | tf_op jit(solution)/shard_map/gathered/pallas_call | solution.py:343
Async XLA Ops:
  2.6 8.8 %copy-start.2 = (f32[5,16,128]{2,1,0:T(8,128)S(1)}, f32[5,16,128]{2,1,0:T(8,128)}, u32[]{:S(2)}) copy-start(f32[5,16,128]{2,1,0:T(8,128)} %get-tuple-element.9) | copy-start | bytes 122884
  2.6 11.9 %collective-permute-start = (f32[5,24,128]{2,1,0:T(8,128)}, f32[5,24,128]{2,1,0:T(8,128)S(1)}, u32[]{:S(2)}, u32[]{:S(2)}) collective-permute-start(f32[5,24,128]{2,1,0:T(8,128)} %get-tuple-element.8.own), channel_id=1, source_target_pairs={{15,0},{0,1},{1,2},{2,3},{3,4},{4,5},{5,6},{6,7},{7,8},{8,9},{9,10... | collective-permute-start | bytes 184328 | tf_op jit(solution)/shard_map/ppermute | solution.py:359
  10.4 0.7 %copy-start.1 = (s32[32]{0:T(128)S(1)}, s32[32]{0:T(128)}, u32[]{:S(2)}) copy-start(s32[32]{0:T(128)} %param.9) | copy-start | bytes 388
  11.4 8.0 %copy-start = (f32[5,24,128]{2,1,0:T(8,128)S(1)}, f32[5,24,128]{2,1,0:T(8,128)}, u32[]{:S(2)}) copy-start(f32[5,24,128]{2,1,0:T(8,128)} %get-tuple-element.8.own) | copy-start | bytes 184324
  11.4 8.0 %collective-permute-start.1 = (f32[5,16,128]{2,1,0:T(8,128)S(1)}, f32[5,16,128]{2,1,0:T(8,128)S(1)}, u32[]{:S(2)}, u32[]{:S(2)}) collective-permute-start(f32[5,16,128]{2,1,0:T(8,128)S(1)} %copy-done.2), channel_id=1, source_target_pairs={{14,0},{15,1},{0,2},{1,3},{2,4},{3,5},{4,6},{5,7},{6,8},{7,9},{8,1... | collective-permute-start | bytes 122888 | tf_op jit(solution)/shard_map/ppermute | solution.py:359

commit v5 on v4

--- a/solution.py
+++ b/solution.py
@@ -11,7 +11,11 @@
 SLICES = 32
 LEAST = 4
 KINDS = K - LEAST + 1
-GROUP = 8
+GROUP1 = 16
+GROUP2 = 16
+GROUP = max(GROUP1, GROUP2)
+PAIRS = GROUP // 2
+HALF = 64
 TM = ("zh", "x", "c")
 SPACE = ("y", "zl")
 
@@ -62,95 +66,134 @@
     return lax.broadcasted_iota(jnp.int32, shape, len(shape) - 1)
 
 
-def slope_planes(planes, beside=None):
-    up, down = row_above(planes), row_below(planes)
-    slopes, sums = [], []
-    for k, plane in enumerate(planes):
-        west, east = left(plane), right(plane)
-        if beside is not None:
-            lane = lanes_of(plane.shape)
-            west, east = jnp.where(lane == 0, beside[k], west), jnp.where(lane == LANES - 1, beside[k], east)
-        slopes.append((down[k] - up[k], east - west))
-        sums.append((up[k] + down[k]) + (west + east))
-    return slopes, sums
-
-
-def fine_groups(table, values, beside, densities, cost, sources, across, along, value_now, density_now, out_value, out_density, spots):
+def paired(a, b):
+    first = lanes_of(a.shape) < HALF
+    return jnp.where(first, a, pltpu.roll(b, HALF, 1)), jnp.where(first, pltpu.roll(a, HALF, 1), b)
+
+
+def pair_planes(many_a, many_b):
+    both = [paired(a, b) for a, b in zip(many_a, many_b)]
+    return [even for even, _ in both], [odd for _, odd in both]
+
+
+def slope_planes(even, odd, beside=None):
+    result = []
+    for parity, planes in enumerate((even, odd)):
+        up, down = row_above(planes), row_below(planes)
+        slopes, sums = [], []
+        for k in range(len(planes)):
+            if parity == 0:
+                west, east = left(odd[k]), odd[k]
+                if beside is not None:
+                    west = jnp.where(lanes_of(west.shape) % HALF == 0, beside[0][k], west)
+            else:
+                west, east = even[k], right(even[k])
+                if beside is not None:
+                    east = jnp.where(lanes_of(east.shape) % HALF == HALF - 1, beside[1][k], east)
+            slopes.append((down[k] - up[k], east - west))
+            sums.append((up[k] + down[k]) + (west + east))
+        result.append((planes, slopes, sums))
+    return result
+
+
+def fine_groups(size, table, values, beside, densities, cost, sources, across, along, value_now, density_now, out_value, out_density, spots):
     (value_at, value_n), (density_at, density_n) = spots
     keep_all, share_all = 1.0 - 4.0 * time_step * diffusion, time_step * diffusion
+    costs = pair_planes(cost, cost)
+    first = lanes_of((8, LANES)) < HALF
 
     def group(number, carry):
-        own = [table[GROUP * number + h] for h in range(GROUP)]
+        own = [table[size * number + h] for h in range(size)]
         trips = [table[SLICES + j] for j in own]
         most = trips[-1]
-        for h in range(GROUP):
-            start = planes_of(values, (own[h],), value_at, value_n)
-            held = planes_of(densities, (own[h],), value_at, value_n)
-            for k in range(value_n):
-                value_now[0][h, k] = value_now[1][h, k] = start[k]
-                sources[h, k] = cost[k] + (0.5 / SCALE * coupling) * held[k]
-            for k, plane in enumerate(planes_of(densities, (own[h],), density_at, density_n)):
-                density_now[0][h, k] = plane
+
+        def taken(ref, at, n, h):
+            return pair_planes(*[planes_of(ref, (own[2 * h + side],), at, n) for side in range(2)])
+
+        def left_at(ref, at, h, both):
+            for side, planes in enumerate(pair_planes(*both)):
+                put_planes(ref, (own[2 * h + side],), at, planes)
+
+        def weights(h, test):
+            on = [test(trips[2 * h + side]) for side in range(2)]
+            keep = jnp.where(first, jnp.where(on[0], keep_all, 1.0), jnp.where(on[1], keep_all, 1.0))
+            share = jnp.where(first, jnp.where(on[0], share_all, 0.0), jnp.where(on[1], share_all, 0.0))
+            return keep, share
+
+        for h in range(size // 2):
+            start, held, density = taken(values, value_at, value_n, h), taken(densities, value_at, value_n, h), taken(densities, density_at, density_n, h)
+            for parity in range(2):
+                for k in range(value_n):
+                    value_now[0][h, parity, k] = value_now[1][h, parity, k] = start[parity][k]
+                    sources[h, parity, k] = costs[parity][k] + (0.5 / SCALE * coupling) * held[parity][k]
+                for k in range(density_n):
+                    density_now[0][h, parity, k] = density[parity][k]
 
         def slopes_of(q, h):
-            now = [value_now[q % 2][h, k] for k in range(value_n)]
-            edges = planes_of(beside, (own[h],), value_at, value_n) if q == 0 and beside is not None else None
-            slopes, sums = slope_planes(now, edges)
-            put_planes(across, (h, q), value_at, [a for a, _ in slopes])
-            put_planes(along, (h, q), value_at, [b for _, b in slopes])
-            return now, slopes, sums
+            now = [[value_now[q % 2][h, parity, k] for k in range(value_n)] for parity in range(2)]
+            edges = taken(beside, value_at, value_n, h) if q == 0 and beside is not None else None
+            result = slope_planes(*now, edges)
+            for parity in range(2):
+                put_planes(across, (2 * h + parity, q), value_at, [a for a, _ in result[parity][1]])
+                put_planes(along, (2 * h + parity, q), value_at, [b for _, b in result[parity][1]])
+            return result
 
         def value_step(q):
-            for h in range(GROUP):
+            for h in range(size // 2):
                 keep, share = keep_all, share_all
                 if q < K - LEAST:
-                    active = q >= K - trips[h]
-                    keep, share = jnp.where(active, keep, 1.0), jnp.where(active, share, 0.0)
-                now, slopes, sums = slopes_of(q, h)
-                for k in range(value_n):
-                    a, b = slopes[k]
-                    value_now[1 - q % 2][h, k] = keep * now[k] + share * (sums[k] + (sources[h, k] - (a * a + b * b)))
+                    keep, share = weights(h, lambda count: q >= K - count)
+                for parity, (now, slopes, sums) in enumerate(slopes_of(q, h)):
+                    for k in range(value_n):
+                        a, b = slopes[k]
+                        value_now[1 - q % 2][h, parity, k] = keep * now[k] + share * (sums[k] + (sources[h, parity, k] - (a * a + b * b)))
 
         def density_step(i):
-            for h in range(GROUP):
+            for h in range(size // 2):
                 keep, share = keep_all, share_all
                 if i >= LEAST:
-                    active = i < trips[h]
-                    keep, share = jnp.where(active, keep, 1.0), jnp.where(active, share, 0.0)
-                a = planes_of(across, (h, K - i), density_at, density_n)
-                b = planes_of(along, (h, K - i), density_at, density_n)
-                here = [density_now[i % 2][h, k] for k in range(density_n)]
-                twice = [plane + plane for plane in here]
-                flux = [twice[k] * a[k] for k in range(density_n)]
-                below = row_below([here[k] + flux[k] for k in range(density_n)])
-                above = row_above([here[k] - flux[k] for k in range(density_n)])
+                    keep, share = weights(h, lambda count: i < count)
+                here, rows, more, less = [], [], [], []
+                for parity in range(2):
+                    a = planes_of(across, (2 * h + parity, K - i), density_at, density_n)
+                    b = planes_of(along, (2 * h + parity, K - i), density_at, density_n)
+                    now = [density_now[i % 2][h, parity, k] for k in range(density_n)]
+                    twice = [plane + plane for plane in now]
+                    flux = [twice[k] * a[k] for k in range(density_n)]
+                    below = row_below([now[k] + flux[k] for k in range(density_n)])
+                    above = row_above([now[k] - flux[k] for k in range(density_n)])
+                    drift = [twice[k] * b[k] for k in range(density_n)]
+                    here.append(now)
+                    rows.append([below[k] + above[k] for k in range(density_n)])
+                    more.append([now[k] + drift[k] for k in range(density_n)])
+                    less.append([now[k] - drift[k] for k in range(density_n)])
                 for k in range(density_n):
-                    drift = twice[k] * b[k]
-                    around = (below[k] + above[k]) + (right(here[k] + drift) + left(here[k] - drift))
-                    density_now[1 - i % 2][h, k] = keep * here[k] + share * around
+                    around = (rows[0][k] + more[1][k]) + left(less[1][k]), (rows[1][k] + less[0][k]) + right(more[0][k])
+                    for parity in range(2):
+                        density_now[1 - i % 2][h, parity, k] = keep * here[parity][k] + share * around[parity]
 
         for q in range(K):
             if q < K - LEAST:
                 pl.when(q >= K - most)(lambda q=q: value_step(q))
             else:
                 value_step(q)
-        for h in range(GROUP):
-            put_planes(out_value, (own[h],), value_at, slopes_of(K, h)[0])
+        for h in range(size // 2):
+            left_at(out_value, value_at, h, [planes for planes, _, _ in slopes_of(K, h)])
         for i in range(K):
             if i >= LEAST:
                 pl.when(i < most)(lambda i=i: density_step(i))
             else:
                 density_step(i)
-        for parity in range(2):
-
-            @pl.when(most % 2 == parity)
-            def _(parity=parity):
-                for h in range(GROUP):
-                    put_planes(out_density, (own[h],), density_at, [density_now[parity][h, k] for k in range(density_n)])
+        for last in range(2):
+
+            @pl.when(most % 2 == last)
+            def _(last=last):
+                for h in range(size // 2):
+                    left_at(out_density, density_at, h, [[density_now[last][h, parity, k] for k in range(density_n)] for parity in range(2)])
 
         return carry
 
-    lax.fori_loop(0, SLICES // GROUP, group, 0)
+    lax.fori_loop(0, SLICES // size, group, 0)
 
 
 def main_kernel(table, own, near, far, message, field, factors, reliefs, cost, m0, u0, e0, m1, u1, fm, fu, across, along, sources, va, vb, da, db):
@@ -193,7 +236,7 @@
 
     lax.fori_loop(0, SLICES, opening, (field[0], field[1] * (1.0 / SCALE), edges[1] * (1.0 / SCALE)), unroll=2)
 
-    fine_groups(table, u0, e0, m0, planes_of(cost, (), 7, 9), sources, across, along, (va, vb), (da, db), fu, fm, ((7, 9), (15, 7)))
+    fine_groups(GROUP1, table, u0, e0, m0, planes_of(cost, (), 7, 9), sources, across, along, (va, vb), (da, db), fu, fm, ((7, 9), (15, 7)))
 
     inner = pl.ds(16, FRAME2)
 
@@ -208,7 +251,7 @@
 
     lax.fori_loop(0, SLICES, first_sweep, (field[0, inner], field[1, inner] * (1.0 / SCALE)), unroll=4)
 
-    fine_groups(table, u1, None, m1, planes_of(cost, (), 23, 5), sources, across, along, (va, vb), (da, db), fu, fm, ((7, 5), (15, 3)))
+    fine_groups(GROUP2, table, u1, None, m1, planes_of(cost, (), 23, 5), sources, across, along, (va, vb), (da, db), fu, fm, ((7, 5), (15, 3)))
 
     tile, wide = pl.ds(24, 8), pl.ds(40, 8)
 
@@ -223,11 +266,13 @@
 
     lax.fori_loop(0, SLICES, second_sweep, (field[0, wide], field[1, wide] * (1.0 / SCALE)), unroll=8)
 
-    first_half = lanes_of((8, LANES)) < 64
+    lane = lanes_of((8, LANES))
+    first_half = lane < HALF
+    wanted = COL_AT // 2 + lane % HALF // 2 + HALF * (lane % 2)
     for j in range(SLICES):
         density, value = m0[j, 0:8], SCALE * u0[j, 0:8]
         ahead, behind = jnp.where(half == 0, density, value), jnp.where(half == 0, value, density)
-        message[j] = jnp.where(first_half, pltpu.roll(ahead, LANES - COL_AT, 1), pltpu.roll(behind, COL_AT, 1))
+        message[j] = jnp.where(first_half, jnp.take_along_axis(ahead, wanted, 1), jnp.take_along_axis(behind, wanted, 1))
 
 
 def place_of():
@@ -255,6 +300,7 @@
         if part < 4:
             a, b = blocks[part, 0], blocks[part, 1]
             window = jnp.where(lane < shift, pltpu.roll(a, shift, 1), pltpu.roll(b, shift, 1))
+            window = jnp.take_along_axis(window, lane % HALF * 2 + lane // HALF, 1)
         else:
             window = beside
         near[part] = window
@@ -322,11 +368,11 @@
         (SLICES, FRAME1, LANES),
         (GROUP, K + 1, FRAME1, LANES),
         (GROUP, K + 1, FRAME1, LANES),
-        (GROUP, 9, 8, LANES),
-        (GROUP, 9, 8, LANES),
-        (GROUP, 9, 8, LANES),
-        (GROUP, 9, 8, LANES),
-        (GROUP, 9, 8, LANES),
+        (PAIRS, 2, 9, 8, LANES),
+        (PAIRS, 2, 9, 8, LANES),
+        (PAIRS, 2, 9, 8, LANES),
+        (PAIRS, 2, 9, 8, LANES),
+        (PAIRS, 2, 9, 8, LANES),
     ]
     return pl.pallas_call(
         main_kernel,

time: 58.8 us -> 57 us (0.969)
  Pallas kernels: 20.4 us -> 18.6 us
    pallas_call x1, Pallas kernels: 17.8 us -> 15.7 us  [both_iterations(): pl.pallas_call(main_kernel, out_shape=f32(SLICES, 8, LANES), in_specs=[sm...]
where the time goes in v5:
time: 57 us; the launch traced here: 56.6 us
  blocking collectives  25.4 us (45%)
  Pallas kernels  18.6 us (33%)
  starting transfers between devices  10.8 us (19%)
  between operations  0.73 us (1%)
  local copies, waits for them, and re-layouts  0.66 us (1%)
    all_to_all x1, blocking collectives, on_device(): received = lax.all_to_all(message, TM, 0, 0, tiled=True)  20.5 us
    pallas_call x1, Pallas kernels, both_iterations(): pl.pallas_call(main_kernel, out_shape=f32(SLICES, 8, LANES), in_specs=[sm...  15.7 us
    ppermute x2, starting transfers between devices, toward_own_side(): return lax.ppermute(array, ('c', *SPACE), hops)  10.8 us
    all_gather x1, blocking collectives, on_device(): near = lax.all_gather(beside, 'c')  4.91 us
    pallas_call x1, Pallas kernels, windows(): pl.pallas_call(window_kernel, out_shape=[f32(PARTS, ROWS, LANES), f32(PAR...  2.22 us
  transfers between devices with their start and end apart: 2, of which 0 were waited for; matrix products, arithmetic and copies ran while one was open for 1% of the time, Pallas kernels for 0%

profile of v5, /device:TPU:1, one launch (start us, length us, event | category | flops | bytes accessed | tf_op | source)
XLA Modules:
  0.0 56.6 jit_solution(1150129549783271439)
XLA Ops:
  0.6 2.2 %windows.1 = (f32[5,24,128]{2,1,0:T(8,128)}, f32[5,16,128]{2,1,0:T(8,128)}) custom-call(f32[24,512]{1,0:T(8,128)} %refs_0_.1, f32[24,512]{1,0:T(8,128)} %refs_1_.1, f32[24,512]{1,0:T(8,128)} %refs_2_.1, f32[24,512]{1,0:T(8,128)} %refs_3_.1), custom_call_target="tpu_custom_call" | custom-call | tf_op jit(solution)/shard_map/windows/pallas_call | solution.py:346
  2.9 0.0 copy-start.2
  2.9 7.7 %collective-permute-start = (f32[5,24,128]{2,1,0:T(8,128)}, f32[5,24,128]{2,1,0:T(8,128)S(1)}, u32[]{:S(2)}, u32[]{:S(2)}) collective-permute-start(f32[5,24,128]{2,1,0:T(8,128)} %get-tuple-element.8.own), channel_id=1, source_target_pairs={{15,0},{0,1},{1,2},{2,3},{3,4},{4,5},{5,6},{6,7},{7,8},{8,9},{9,10... | collective-permute-start | bytes 184328 | tf_op jit(solution)/shard_map/ppermute | solution.py:405
  10.6 0.0 copy-start.1
  10.6 0.6 %copy-done.1 = s32[32]{0:T(128)S(1)} copy-done((s32[32]{0:T(128)S(1)}, s32[32]{0:T(128)}, u32[]{:S(2)}) %copy-start.1) | copy-done | bytes 152
  11.3 0.2 convert_reduce_fusion
  11.5 0.1 select_reduce_fusion
  11.6 0.1 pad_add_fusion.table
  11.7 0.0 copy-done.2
  11.7 0.0 copy-start
  11.7 3.1 %collective-permute-start.1 = (f32[5,16,128]{2,1,0:T(8,128)S(1)}, f32[5,16,128]{2,1,0:T(8,128)S(1)}, u32[]{:S(2)}, u32[]{:S(2)}) collective-permute-start(f32[5,16,128]{2,1,0:T(8,128)S(1)} %copy-done.2), channel_id=1, source_target_pairs={{14,0},{15,1},{0,2},{1,3},{2,4},{3,5},{4,6},{5,7},{6,8},{7,9},{8,1... | collective-permute-start | bytes 122888 | tf_op jit(solution)/shard_map/ppermute | solution.py:405
  14.8 0.0 collective-permute-done
  14.8 4.9 %all-gather = f32[10,24,128]{2,1,0:T(8,128)S(1)} all-gather(f32[5,24,128]{2,1,0:T(8,128)S(1)} %collective-permute-done), channel_id=2, replica_groups=mesh['zh'=4,'x'=4,'c'=2,'y'=8,'zl'=2] {'c'}, dimensions={0}, use_global_device_ids=true | all-gather | bytes 184320 | tf_op jit(solution)/shard_map/all_gather | solution.py:411
  19.7 0.0 collective-permute-done.1.far
  19.7 0.0 copy-done
  19.7 15.7 %both_iterations.1 = f32[32,8,128]{2,1,0:T(8,128)S(1)} custom-call(s32[66]{0:T(128)S(1)} %pad_add_fusion.table, f32[5,24,128]{2,1,0:T(8,128)S(1)} %copy-done, f32[2,5,24,128]{3,2,1,0:T(8,128)S(1)} %bitcast.3, f32[5,16,128]{2,1,0:T(8,128)S(1)} %collective-permute-done.1.far), custom_call_target="tpu_custom_call" | custom-call | tf_op jit(solution)/shard_map/both_iterations/pallas_call | solution.py:377
  35.4 20.5 %all_to_all.5.received = f32[32,8,128]{2,1,0:T(8,128)S(1)} all-to-all(f32[32,8,128]{2,1,0:T(8,128)S(1)} %both_iterations.1), channel_id=1, replica_groups=mesh['zh'=4,'x'=4,'c'=2,'y'=8,'zl'=2] {'zh','x','c'}, dimensions={0} | all-to-all | bytes 262144 | tf_op jit(solution)/shard_map/all_to_all | solution.py:421
  55.9 0.7 %gathered.1 = (f32[1,24,512]{2,1,0:T(8,128)}, f32[1,24,512]{2,1,0:T(8,128)}) custom-call(f32[32,8,128]{2,1,0:T(8,128)S(1)} %all_to_all.5.received), custom_call_target="tpu_custom_call" | custom-call | tf_op jit(solution)/shard_map/gathered/pallas_call | solution.py:389
Async XLA Ops:
  2.9 8.8 %copy-start.2 = (f32[5,16,128]{2,1,0:T(8,128)S(1)}, f32[5,16,128]{2,1,0:T(8,128)}, u32[]{:S(2)}) copy-start(f32[5,16,128]{2,1,0:T(8,128)} %get-tuple-element.9) | copy-start | bytes 122884
  2.9 11.9 %collective-permute-start = (f32[5,24,128]{2,1,0:T(8,128)}, f32[5,24,128]{2,1,0:T(8,128)S(1)}, u32[]{:S(2)}, u32[]{:S(2)}) collective-permute-start(f32[5,24,128]{2,1,0:T(8,128)} %get-tuple-element.8.own), channel_id=1, source_target_pairs={{15,0},{0,1},{1,2},{2,3},{3,4},{4,5},{5,6},{6,7},{7,8},{8,9},{9,10... | collective-permute-start | bytes 184328 | tf_op jit(solution)/shard_map/ppermute | solution.py:405
  10.6 0.7 %copy-start.1 = (s32[32]{0:T(128)S(1)}, s32[32]{0:T(128)}, u32[]{:S(2)}) copy-start(s32[32]{0:T(128)} %param.9) | copy-start | bytes 388
  11.7 8.0 %copy-start = (f32[5,24,128]{2,1,0:T(8,128)S(1)}, f32[5,24,128]{2,1,0:T(8,128)}, u32[]{:S(2)}) copy-start(f32[5,24,128]{2,1,0:T(8,128)} %get-tuple-element.8.own) | copy-start | bytes 184324
  11.7 8.0 %collective-permute-start.1 = (f32[5,16,128]{2,1,0:T(8,128)S(1)}, f32[5,16,128]{2,1,0:T(8,128)S(1)}, u32[]{:S(2)}, u32[]{:S(2)}) collective-permute-start(f32[5,16,128]{2,1,0:T(8,128)S(1)} %copy-done.2), channel_id=1, source_target_pairs={{14,0},{15,1},{0,2},{1,3},{2,4},{3,5},{4,6},{5,7},{6,8},{7,9},{8,1... | collective-permute-start | bytes 122888 | tf_op jit(solution)/shard_map/ppermute | solution.py:405

commit v6 on v5

--- a/solution.py
+++ b/solution.py
@@ -272,7 +272,8 @@
     for j in range(SLICES):
         density, value = m0[j, 0:8], SCALE * u0[j, 0:8]
         ahead, behind = jnp.where(half == 0, density, value), jnp.where(half == 0, value, density)
-        message[j] = jnp.where(first_half, jnp.take_along_axis(ahead, wanted, 1), jnp.take_along_axis(behind, wanted, 1))
+        whole = jnp.where(first_half, jnp.take_along_axis(ahead, wanted, 1), jnp.take_along_axis(behind, wanted, 1))
+        message[j] = whole[0:TILE_ROWS]
 
 
 def place_of():
@@ -320,14 +321,14 @@
 
 
 def gather_kernel(received, density, value):
-    first_half = lanes_of((8, LANES)) < 64
+    first_half = lanes_of((TILE_ROWS, LANES)) < 64
     for zh in range(4):
         for band in range(4):
             at = [zh * 8 + (2 * half + band % 2) * 2 + band // 2 for half in range(2)]
             a, b = received[at[0]], received[at[1]]
             rows, lanes = slice(TILE_ROWS * band, TILE_ROWS * (band + 1)), slice(LANES * zh, LANES * (zh + 1))
-            density[0, rows, lanes] = jnp.where(first_half, a, b)[0:TILE_ROWS]
-            value[0, rows, lanes] = pltpu.roll(jnp.where(first_half, b, a), 64, 1)[0:TILE_ROWS]
+            density[0, rows, lanes] = jnp.where(first_half, a, b)
+            value[0, rows, lanes] = pltpu.roll(jnp.where(first_half, b, a), 64, 1)
 
 
 def vmem():
@@ -376,7 +377,7 @@
     ]
     return pl.pallas_call(
         main_kernel,
-        out_shape=f32(SLICES, 8, LANES),
+        out_shape=f32(SLICES, TILE_ROWS, LANES),
         in_specs=[smem(), vmem(), vmem(), vmem()],
         out_specs=vmem(),
         scratch_shapes=[pltpu.VMEM(shape, jnp.float32) for shape in scratch],

time: 57 us -> 57.8 us (1.014)
  Pallas kernels: 18.6 us -> 19.4 us
    pallas_call x1, Pallas kernels: 15.7 us -> 16.5 us  [both_iterations(): pl.pallas_call(main_kernel, out_shape=f32(SLICES, TILE_ROWS, LANES), in_s...]
where the time goes in v6:
time: 57.8 us; the launch traced here: 57.5 us
  blocking collectives  25.4 us (44%)
  Pallas kernels  19.4 us (34%)
  starting transfers between devices  10.8 us (19%)
  between operations  0.73 us (1%)
  local copies, waits for them, and re-layouts  0.66 us (1%)
    all_to_all x1, blocking collectives, on_device(): received = lax.all_to_all(message, TM, 0, 0, tiled=True)  20.5 us
    pallas_call x1, Pallas kernels, both_iterations(): pl.pallas_call(main_kernel, out_shape=f32(SLICES, TILE_ROWS, LANES), in_s...  16.5 us
    ppermute x2, starting transfers between devices, toward_own_side(): return lax.ppermute(array, ('c', *SPACE), hops)  10.8 us
    all_gather x1, blocking collectives, on_device(): near = lax.all_gather(beside, 'c')  4.91 us
    pallas_call x1, Pallas kernels, windows(): pl.pallas_call(window_kernel, out_shape=[f32(PARTS, ROWS, LANES), f32(PAR...  2.22 us
  transfers between devices with their start and end apart: 2, of which 0 were waited for; matrix products, arithmetic and copies ran while one was open for 1% of the time, Pallas kernels for 0%

profile of v6, /device:TPU:1, one launch (start us, length us, event | category | flops | bytes accessed | tf_op | source)
XLA Modules:
  0.0 57.5 jit_solution(6471588392255937785)
XLA Ops:
  0.6 2.2 %windows.1 = (f32[5,24,128]{2,1,0:T(8,128)}, f32[5,16,128]{2,1,0:T(8,128)}) custom-call(f32[24,512]{1,0:T(8,128)} %refs_0_.1, f32[24,512]{1,0:T(8,128)} %refs_1_.1, f32[24,512]{1,0:T(8,128)} %refs_2_.1, f32[24,512]{1,0:T(8,128)} %refs_3_.1), custom_call_target="tpu_custom_call" | custom-call | tf_op jit(solution)/shard_map/windows/pallas_call | solution.py:347
  2.9 0.0 copy-start.2
  2.9 7.7 %collective-permute-start = (f32[5,24,128]{2,1,0:T(8,128)}, f32[5,24,128]{2,1,0:T(8,128)S(1)}, u32[]{:S(2)}, u32[]{:S(2)}) collective-permute-start(f32[5,24,128]{2,1,0:T(8,128)} %get-tuple-element.8.own), channel_id=1, source_target_pairs={{15,0},{0,1},{1,2},{2,3},{3,4},{4,5},{5,6},{6,7},{7,8},{8,9},{9,10... | collective-permute-start | bytes 184328 | tf_op jit(solution)/shard_map/ppermute | solution.py:406
  10.6 0.0 copy-start.1
  10.6 0.6 %copy-done.1 = s32[32]{0:T(128)S(1)} copy-done((s32[32]{0:T(128)S(1)}, s32[32]{0:T(128)}, u32[]{:S(2)}) %copy-start.1) | copy-done | bytes 152
  11.3 0.2 convert_reduce_fusion
  11.5 0.1 select_reduce_fusion
  11.6 0.1 pad_add_fusion.table
  11.7 0.0 copy-done.2
  11.7 0.0 copy-start
  11.7 3.1 %collective-permute-start.1 = (f32[5,16,128]{2,1,0:T(8,128)S(1)}, f32[5,16,128]{2,1,0:T(8,128)S(1)}, u32[]{:S(2)}, u32[]{:S(2)}) collective-permute-start(f32[5,16,128]{2,1,0:T(8,128)S(1)} %copy-done.2), channel_id=1, source_target_pairs={{14,0},{15,1},{0,2},{1,3},{2,4},{3,5},{4,6},{5,7},{6,8},{7,9},{8,1... | collective-permute-start | bytes 122888 | tf_op jit(solution)/shard_map/ppermute | solution.py:406
  14.8 0.0 collective-permute-done
  14.8 4.9 %all-gather = f32[10,24,128]{2,1,0:T(8,128)S(1)} all-gather(f32[5,24,128]{2,1,0:T(8,128)S(1)} %collective-permute-done), channel_id=2, replica_groups=mesh['zh'=4,'x'=4,'c'=2,'y'=8,'zl'=2] {'c'}, dimensions={0}, use_global_device_ids=true | all-gather | bytes 184320 | tf_op jit(solution)/shard_map/all_gather | solution.py:412
  19.7 0.0 collective-permute-done.1.far
  19.7 0.0 copy-done
  19.7 16.5 %both_iterations.1 = f32[32,6,128]{2,1,0:T(8,128)S(1)} custom-call(s32[66]{0:T(128)S(1)} %pad_add_fusion.table, f32[5,24,128]{2,1,0:T(8,128)S(1)} %copy-done, f32[2,5,24,128]{3,2,1,0:T(8,128)S(1)} %bitcast.3, f32[5,16,128]{2,1,0:T(8,128)S(1)} %collective-permute-done.1.far), custom_call_target="tpu_custom_call" | custom-call | tf_op jit(solution)/shard_map/both_iterations/pallas_call | solution.py:378
  36.2 20.5 %all_to_all.5.received = f32[32,6,128]{2,1,0:T(8,128)S(1)} all-to-all(f32[32,6,128]{2,1,0:T(8,128)S(1)} %both_iterations.1), channel_id=1, replica_groups=mesh['zh'=4,'x'=4,'c'=2,'y'=8,'zl'=2] {'zh','x','c'}, dimensions={0} | all-to-all | bytes 196608 | tf_op jit(solution)/shard_map/all_to_all | solution.py:422
  56.8 0.7 %gathered.1 = (f32[1,24,512]{2,1,0:T(8,128)}, f32[1,24,512]{2,1,0:T(8,128)}) custom-call(f32[32,6,128]{2,1,0:T(8,128)S(1)} %all_to_all.5.received), custom_call_target="tpu_custom_call" | custom-call | tf_op jit(solution)/shard_map/gathered/pallas_call | solution.py:390
Async XLA Ops:
  2.9 8.8 %copy-start.2 = (f32[5,16,128]{2,1,0:T(8,128)S(1)}, f32[5,16,128]{2,1,0:T(8,128)}, u32[]{:S(2)}) copy-start(f32[5,16,128]{2,1,0:T(8,128)} %get-tuple-element.9) | copy-start | bytes 122884
  2.9 11.9 %collective-permute-start = (f32[5,24,128]{2,1,0:T(8,128)}, f32[5,24,128]{2,1,0:T(8,128)S(1)}, u32[]{:S(2)}, u32[]{:S(2)}) collective-permute-start(f32[5,24,128]{2,1,0:T(8,128)} %get-tuple-element.8.own), channel_id=1, source_target_pairs={{15,0},{0,1},{1,2},{2,3},{3,4},{4,5},{5,6},{6,7},{7,8},{8,9},{9,10... | collective-permute-start | bytes 184328 | tf_op jit(solution)/shard_map/ppermute | solution.py:406
  10.6 0.7 %copy-start.1 = (s32[32]{0:T(128)S(1)}, s32[32]{0:T(128)}, u32[]{:S(2)}) copy-start(s32[32]{0:T(128)} %param.9) | copy-start | bytes 388
  11.7 8.0 %copy-start = (f32[5,24,128]{2,1,0:T(8,128)S(1)}, f32[5,24,128]{2,1,0:T(8,128)}, u32[]{:S(2)}) copy-start(f32[5,24,128]{2,1,0:T(8,128)} %get-tuple-element.8.own) | copy-start | bytes 184324
  11.7 8.0 %collective-permute-start.1 = (f32[5,16,128]{2,1,0:T(8,128)S(1)}, f32[5,16,128]{2,1,0:T(8,128)S(1)}, u32[]{:S(2)}, u32[]{:S(2)}) collective-permute-start(f32[5,16,128]{2,1,0:T(8,128)S(1)} %copy-done.2), channel_id=1, source_target_pairs={{14,0},{15,1},{0,2},{1,3},{2,4},{3,5},{4,6},{5,7},{6,8},{7,9},{8,1... | collective-permute-start | bytes 122888 | tf_op jit(solution)/shard_map/ppermute | solution.py:406

commit v7 on v6

--- a/solution.py
+++ b/solution.py
@@ -414,9 +414,9 @@
     numbers = jnp.arange(SLICES, dtype=jnp.int32)
     ahead = (slice_steps[None, :] < slice_steps[:, None]) | ((slice_steps[None, :] == slice_steps[:, None]) & (numbers[None, :] < numbers[:, None]))
     rank = jnp.sum(ahead.astype(jnp.int32), axis=1)
+    edge, rank = lax.optimization_barrier((edge, rank))
     order = jnp.sum(jnp.where(rank[None, :] == numbers[:, None], numbers[None, :], 0), axis=1)
     table = jnp.concatenate([order, slice_steps, jnp.stack([band, half]).astype(jnp.int32)])
-    edge, table = lax.optimization_barrier((edge, table))
     far = toward_own_side(edge, 2)
     message = both_iterations(table, own, near, far)
     received = lax.all_to_all(message, TM, 0, 0, tiled=True)

time: 57.8 us -> 60 us (1.038)
  blocking collectives: 25.4 us -> 26.4 us
  other arithmetic: 0.37 us -> 1.1 us
  waiting for transfers between devices: 0.01 us -> 0.71 us
    all_gather x1, blocking collectives: 4.91 us -> 6.46 us  [on_device(): near = lax.all_gather(beside, 'c')]
    reduce_sum x1, other arithmetic: 0.18 us -> 0.91 us  [on_device(): rank = jnp.sum(ahead.astype(jnp.int32), axis=1)]
    ppermute x2, waiting for transfers between devices: 0.01 us -> 0.71 us  [toward_own_side(): return lax.ppermute(array, ('c', *SPACE), hops)]
    all_to_all x1, blocking collectives: 20.5 us -> 19.9 us  [on_device(): received = lax.all_to_all(message, TM, 0, 0, tiled=True)]
  transfers between devices with their start and end apart: 2 -> 2, of which waited for: 0 -> 1; matrix products, arithmetic and copies ran while one was open for 1% -> 0% of each run, Pallas kernels for 0% -> 0%
where the time goes in v7:
time: 60 us; the launch traced here: 59.7 us
  blocking collectives  26.4 us (44%)
  Pallas kernels  19.5 us (32%)
  starting transfers between devices  10.7 us (18%)
  other arithmetic  1.1 us (2%)
  waiting for transfers between devices  0.71 us (1%)
  between operations  0.71 us (1%)
  local copies, waits for them, and re-layouts  0.65 us (1%)
    all_to_all x1, blocking collectives, on_device(): received = lax.all_to_all(message, TM, 0, 0, tiled=True)  19.9 us
    pallas_call x1, Pallas kernels, both_iterations(): pl.pallas_call(main_kernel, out_shape=f32(SLICES, TILE_ROWS, LANES), in_s...  16.5 us
    ppermute x2, starting transfers between devices, toward_own_side(): return lax.ppermute(array, ('c', *SPACE), hops)  10.7 us
    all_gather x1, blocking collectives, on_device(): near = lax.all_gather(beside, 'c')  6.46 us
    pallas_call x1, Pallas kernels, windows(): pl.pallas_call(window_kernel, out_shape=[f32(PARTS, ROWS, LANES), f32(PAR...  2.22 us
  transfers between devices with their start and end apart: 2, of which 1 were waited for; matrix products, arithmetic and copies ran while one was open for 0% of the time, Pallas kernels for 0%

profile of v7, /device:TPU:1, one launch (start us, length us, event | category | flops | bytes accessed | tf_op | source)
XLA Modules:
  0.0 59.7 jit_solution(1897798634830473752)
XLA Ops:
  0.6 0.9 %convert_reduce_fusion = s32[32]{0:T(128)S(1)} fusion(s32[32]{0:T(128)} %param.9), kind=kLoop, calls=%fused_computation.2 | loop fusion | flops 7136 | bytes 256 | tf_op jit(solution)/shard_map/reduce_sum | solution.py:416
  1.5 2.2 %windows.1 = (f32[5,24,128]{2,1,0:T(8,128)}, f32[5,16,128]{2,1,0:T(8,128)}) custom-call(f32[24,512]{1,0:T(8,128)} %refs_0_.1, f32[24,512]{1,0:T(8,128)} %refs_1_.1, f32[24,512]{1,0:T(8,128)} %refs_2_.1, f32[24,512]{1,0:T(8,128)} %refs_3_.1), custom_call_target="tpu_custom_call" | custom-call | tf_op jit(solution)/shard_map/windows/pallas_call | solution.py:347
  3.8 5.9 %collective-permute-start.1 = (f32[5,16,128]{2,1,0:T(8,128)}, f32[5,16,128]{2,1,0:T(8,128)S(1)}, u32[]{:S(2)}, u32[]{:S(2)}) collective-permute-start(f32[5,16,128]{2,1,0:T(8,128)} %get-tuple-element.9), channel_id=1, source_target_pairs={{14,0},{15,1},{0,2},{1,3},{2,4},{3,5},{4,6},{5,7},{6,8},{7,9},{8,1... | collective-permute-start | bytes 122888 | tf_op jit(solution)/shard_map/ppermute | solution.py:406
  9.7 4.8 %collective-permute-start = (f32[5,24,128]{2,1,0:T(8,128)}, f32[5,24,128]{2,1,0:T(8,128)S(1)}, u32[]{:S(2)}, u32[]{:S(2)}) collective-permute-start(f32[5,24,128]{2,1,0:T(8,128)} %get-tuple-element.8.own), channel_id=1, source_target_pairs={{15,0},{0,1},{1,2},{2,3},{3,4},{4,5},{5,6},{6,7},{7,8},{8,9},{9,10... | collective-permute-start | bytes 184328 | tf_op jit(solution)/shard_map/ppermute | solution.py:406
  14.5 0.1 select_reduce_fusion
  14.6 0.0 copy-start.1
  14.7 0.6 %copy-done.1 = s32[32]{0:T(128)S(1)} copy-done((s32[32]{0:T(128)S(1)}, s32[32]{0:T(128)}, u32[]{:S(2)}) %copy-start.1) | copy-done | bytes 152
  15.3 0.1 pad_add_fusion.table
  15.4 0.0 copy-start
  15.4 0.7 %collective-permute-done = f32[5,24,128]{2,1,0:T(8,128)S(1)} collective-permute-done((f32[5,24,128]{2,1,0:T(8,128)}, f32[5,24,128]{2,1,0:T(8,128)S(1)}, u32[]{:S(2)}, u32[]{:S(2)}) %collective-permute-start) | collective-permute-done | bytes 61472 | tf_op jit(solution)/shard_map/ppermute | solution.py:406
  16.1 6.5 %all-gather = f32[10,24,128]{2,1,0:T(8,128)S(1)} all-gather(f32[5,24,128]{2,1,0:T(8,128)S(1)} %collective-permute-done), channel_id=2, replica_groups=mesh['zh'=4,'x'=4,'c'=2,'y'=8,'zl'=2] {'c'}, dimensions={0}, use_global_device_ids=true | all-gather | bytes 184320 | tf_op jit(solution)/shard_map/all_gather | solution.py:412
  22.5 0.0 collective-permute-done.1.far
  22.5 0.0 copy-done
  22.5 16.5 %both_iterations.1 = f32[32,6,128]{2,1,0:T(8,128)S(1)} custom-call(s32[66]{0:T(128)S(1)} %pad_add_fusion.table, f32[5,24,128]{2,1,0:T(8,128)S(1)} %copy-done, f32[2,5,24,128]{3,2,1,0:T(8,128)S(1)} %bitcast.3, f32[5,16,128]{2,1,0:T(8,128)S(1)} %collective-permute-done.1.far), custom_call_target="tpu_custom_call" | custom-call | tf_op jit(solution)/shard_map/both_iterations/pallas_call | solution.py:378
  39.1 19.9 %all_to_all.5.received = f32[32,6,128]{2,1,0:T(8,128)S(1)} all-to-all(f32[32,6,128]{2,1,0:T(8,128)S(1)} %both_iterations.1), channel_id=1, replica_groups=mesh['zh'=4,'x'=4,'c'=2,'y'=8,'zl'=2] {'zh','x','c'}, dimensions={0} | all-to-all | bytes 196608 | tf_op jit(solution)/shard_map/all_to_all | solution.py:422
  59.0 0.7 %gathered.1 = (f32[1,24,512]{2,1,0:T(8,128)}, f32[1,24,512]{2,1,0:T(8,128)}) custom-call(f32[32,6,128]{2,1,0:T(8,128)S(1)} %all_to_all.5.received), custom_call_target="tpu_custom_call" | custom-call | tf_op jit(solution)/shard_map/gathered/pallas_call | solution.py:390
Async XLA Ops:
  3.8 18.8 %collective-permute-start.1 = (f32[5,16,128]{2,1,0:T(8,128)}, f32[5,16,128]{2,1,0:T(8,128)S(1)}, u32[]{:S(2)}, u32[]{:S(2)}) collective-permute-start(f32[5,16,128]{2,1,0:T(8,128)} %get-tuple-element.9), channel_id=1, source_target_pairs={{14,0},{15,1},{0,2},{1,3},{2,4},{3,5},{4,6},{5,7},{6,8},{7,9},{8,1... | collective-permute-start | bytes 122888 | tf_op jit(solution)/shard_map/ppermute | solution.py:406
  9.7 6.4 %collective-permute-start = (f32[5,24,128]{2,1,0:T(8,128)}, f32[5,24,128]{2,1,0:T(8,128)S(1)}, u32[]{:S(2)}, u32[]{:S(2)}) collective-permute-start(f32[5,24,128]{2,1,0:T(8,128)} %get-tuple-element.8.own), channel_id=1, source_target_pairs={{15,0},{0,1},{1,2},{2,3},{3,4},{4,5},{5,6},{6,7},{7,8},{8,9},{9,10... | collective-permute-start | bytes 184328 | tf_op jit(solution)/shard_map/ppermute | solution.py:406
  14.6 0.7 %copy-start.1 = (s32[32]{0:T(128)S(1)}, s32[32]{0:T(128)}, u32[]{:S(2)}) copy-start(s32[32]{0:T(128)} %param.9) | copy-start | bytes 388
  15.4 7.2 %copy-start = (f32[5,24,128]{2,1,0:T(8,128)S(1)}, f32[5,24,128]{2,1,0:T(8,128)}, u32[]{:S(2)}) copy-start(f32[5,24,128]{2,1,0:T(8,128)} %get-tuple-element.8.own) | copy-start | bytes 184324

commit v8 on v6

--- a/solution.py
+++ b/solution.py
@@ -293,15 +293,16 @@
             copies.append(pltpu.make_async_copy(array.at[:, pl.ds(at, LANES)], blocks.at[part, which], arrived.at[part, which]))
     for copy in copies:
         copy.start()
-    for copy in copies:
-        copy.wait()
     lane = lanes_of((ROWS, LANES))
+    column_in = lane % HALF * 2 + lane // HALF
+    lane_of_it = (column_in + LANES - shift) % LANES
     beside = jnp.zeros((ROWS, LANES), jnp.float32)
     for part in range(PARTS):
         if part < 4:
+            for copy in copies[2 * part : 2 * part + 2]:
+                copy.wait()
             a, b = blocks[part, 0], blocks[part, 1]
-            window = jnp.where(lane < shift, pltpu.roll(a, shift, 1), pltpu.roll(b, shift, 1))
-            window = jnp.take_along_axis(window, lane % HALF * 2 + lane // HALF, 1)
+            window = jnp.where(column_in < shift, jnp.take_along_axis(a, lane_of_it, 1), jnp.take_along_axis(b, lane_of_it, 1))
         else:
             window = beside
         near[part] = window

time: 57.8 us -> 57.6 us (level)
  no operation moved by 1% of the time
where the time goes in v8:
time: 57.6 us; the launch traced here: 57.3 us
  blocking collectives  25.4 us (44%)
  Pallas kernels  19.2 us (33%)
  starting transfers between devices  10.8 us (19%)
  between operations  0.73 us (1%)
  local copies, waits for them, and re-layouts  0.66 us (1%)
    all_to_all x1, blocking collectives, on_device(): received = lax.all_to_all(message, TM, 0, 0, tiled=True)  20.5 us
    pallas_call x1, Pallas kernels, both_iterations(): pl.pallas_call(main_kernel, out_shape=f32(SLICES, TILE_ROWS, LANES), in_s...  16.5 us
    ppermute x2, starting transfers between devices, toward_own_side(): return lax.ppermute(array, ('c', *SPACE), hops)  10.8 us
    all_gather x1, blocking collectives, on_device(): near = lax.all_gather(beside, 'c')  4.91 us
    pallas_call x1, Pallas kernels, windows(): pl.pallas_call(window_kernel, out_shape=[f32(PARTS, ROWS, LANES), f32(PAR...  2 us
  transfers between devices with their start and end apart: 2, of which 0 were waited for; matrix products, arithmetic and copies ran while one was open for 1% of the time, Pallas kernels for 0%

profile of v8, /device:TPU:1, one launch (start us, length us, event | category | flops | bytes accessed | tf_op | source)
XLA Modules:
  0.0 57.3 jit_solution(2316312136319453021)
XLA Ops:
  0.6 2.0 %windows.1 = (f32[5,24,128]{2,1,0:T(8,128)}, f32[5,16,128]{2,1,0:T(8,128)}) custom-call(f32[24,512]{1,0:T(8,128)} %refs_0_.1, f32[24,512]{1,0:T(8,128)} %refs_1_.1, f32[24,512]{1,0:T(8,128)} %refs_2_.1, f32[24,512]{1,0:T(8,128)} %refs_3_.1), custom_call_target="tpu_custom_call" | custom-call | tf_op jit(solution)/shard_map/windows/pallas_call | solution.py:348
  2.6 0.0 copy-start.2
  2.6 7.7 %collective-permute-start = (f32[5,24,128]{2,1,0:T(8,128)}, f32[5,24,128]{2,1,0:T(8,128)S(1)}, u32[]{:S(2)}, u32[]{:S(2)}) collective-permute-start(f32[5,24,128]{2,1,0:T(8,128)} %get-tuple-element.8.own), channel_id=1, source_target_pairs={{15,0},{0,1},{1,2},{2,3},{3,4},{4,5},{5,6},{6,7},{7,8},{8,9},{9,10... | collective-permute-start | bytes 184328 | tf_op jit(solution)/shard_map/ppermute | solution.py:407
  10.4 0.0 copy-start.1
  10.4 0.6 %copy-done.1 = s32[32]{0:T(128)S(1)} copy-done((s32[32]{0:T(128)S(1)}, s32[32]{0:T(128)}, u32[]{:S(2)}) %copy-start.1) | copy-done | bytes 152
  11.1 0.2 convert_reduce_fusion
  11.2 0.1 select_reduce_fusion
  11.4 0.1 pad_add_fusion.table
  11.5 0.0 copy-done.2
  11.5 0.0 copy-start
  11.5 3.1 %collective-permute-start.1 = (f32[5,16,128]{2,1,0:T(8,128)S(1)}, f32[5,16,128]{2,1,0:T(8,128)S(1)}, u32[]{:S(2)}, u32[]{:S(2)}) collective-permute-start(f32[5,16,128]{2,1,0:T(8,128)S(1)} %copy-done.2), channel_id=1, source_target_pairs={{14,0},{15,1},{0,2},{1,3},{2,4},{3,5},{4,6},{5,7},{6,8},{7,9},{8,1... | collective-permute-start | bytes 122888 | tf_op jit(solution)/shard_map/ppermute | solution.py:407
  14.6 0.0 collective-permute-done
  14.6 4.9 %all-gather = f32[10,24,128]{2,1,0:T(8,128)S(1)} all-gather(f32[5,24,128]{2,1,0:T(8,128)S(1)} %collective-permute-done), channel_id=2, replica_groups=mesh['zh'=4,'x'=4,'c'=2,'y'=8,'zl'=2] {'c'}, dimensions={0}, use_global_device_ids=true | all-gather | bytes 184320 | tf_op jit(solution)/shard_map/all_gather | solution.py:413
  19.5 0.0 collective-permute-done.1.far
  19.5 0.0 copy-done
  19.5 16.5 %both_iterations.1 = f32[32,6,128]{2,1,0:T(8,128)S(1)} custom-call(s32[66]{0:T(128)S(1)} %pad_add_fusion.table, f32[5,24,128]{2,1,0:T(8,128)S(1)} %copy-done, f32[2,5,24,128]{3,2,1,0:T(8,128)S(1)} %bitcast.3, f32[5,16,128]{2,1,0:T(8,128)S(1)} %collective-permute-done.1.far), custom_call_target="tpu_custom_call" | custom-call | tf_op jit(solution)/shard_map/both_iterations/pallas_call | solution.py:379
  36.0 20.5 %all_to_all.5.received = f32[32,6,128]{2,1,0:T(8,128)S(1)} all-to-all(f32[32,6,128]{2,1,0:T(8,128)S(1)} %both_iterations.1), channel_id=1, replica_groups=mesh['zh'=4,'x'=4,'c'=2,'y'=8,'zl'=2] {'zh','x','c'}, dimensions={0} | all-to-all | bytes 196608 | tf_op jit(solution)/shard_map/all_to_all | solution.py:423
  56.5 0.7 %gathered.1 = (f32[1,24,512]{2,1,0:T(8,128)}, f32[1,24,512]{2,1,0:T(8,128)}) custom-call(f32[32,6,128]{2,1,0:T(8,128)S(1)} %all_to_all.5.received), custom_call_target="tpu_custom_call" | custom-call | tf_op jit(solution)/shard_map/gathered/pallas_call | solution.py:391
Async XLA Ops:
  2.6 8.8 %copy-start.2 = (f32[5,16,128]{2,1,0:T(8,128)S(1)}, f32[5,16,128]{2,1,0:T(8,128)}, u32[]{:S(2)}) copy-start(f32[5,16,128]{2,1,0:T(8,128)} %get-tuple-element.9) | copy-start | bytes 122884
  2.6 11.9 %collective-permute-start = (f32[5,24,128]{2,1,0:T(8,128)}, f32[5,24,128]{2,1,0:T(8,128)S(1)}, u32[]{:S(2)}, u32[]{:S(2)}) collective-permute-start(f32[5,24,128]{2,1,0:T(8,128)} %get-tuple-element.8.own), channel_id=1, source_target_pairs={{15,0},{0,1},{1,2},{2,3},{3,4},{4,5},{5,6},{6,7},{7,8},{8,9},{9,10... | collective-permute-start | bytes 184328 | tf_op jit(solution)/shard_map/ppermute | solution.py:407
  10.4 0.7 %copy-start.1 = (s32[32]{0:T(128)S(1)}, s32[32]{0:T(128)}, u32[]{:S(2)}) copy-start(s32[32]{0:T(128)} %param.9) | copy-start | bytes 388
  11.5 8.0 %copy-start = (f32[5,24,128]{2,1,0:T(8,128)S(1)}, f32[5,24,128]{2,1,0:T(8,128)}, u32[]{:S(2)}) copy-start(f32[5,24,128]{2,1,0:T(8,128)} %get-tuple-element.8.own) | copy-start | bytes 184324
  11.5 8.0 %collective-permute-start.1 = (f32[5,16,128]{2,1,0:T(8,128)S(1)}, f32[5,16,128]{2,1,0:T(8,128)S(1)}, u32[]{:S(2)}, u32[]{:S(2)}) collective-permute-start(f32[5,16,128]{2,1,0:T(8,128)S(1)} %copy-done.2), channel_id=1, source_target_pairs={{14,0},{15,1},{0,2},{1,3},{2,4},{3,5},{4,6},{5,7},{6,8},{7,9},{8,1... | collective-permute-start | bytes 122888 | tf_op jit(solution)/shard_map/ppermute | solution.py:407
